TPU v7x, 32 devices: a whole 2x2x4 slice. The times are simulated.
32 devices in a mesh: dp: 16 (over z, y, x), tensor: 2 (over core).
Axes of the slice: x: 2, y: 2, z: 4, core: 2. Of those that a mesh axis runs over, the one named last changes fastest.
Arguments:
- query_in: bfloat16 [24576, 4096], P('dp', 'tensor'), may hold values from -6 to 6
- key_in: bfloat16 [24576, 4096], P('dp', 'tensor'), may hold values from -6 to 6
- value_in: bfloat16 [24576, 4096], P('dp', 'tensor'), may hold values from -6 to 6
- feat_filter: float32 [3, 7, 4096], P(None, None, 'tensor'), may hold values from -2.5 to 2.5
- inner_filter: float32 [7, 4096], P(None, 'tensor'), may hold values from -2.5 to 2.5
- out_weight: bfloat16 [4096, 4096], P('tensor'), may hold values from -0.125 to 0.125
- doc_pos: int32 [24576], P('dp'), may hold values from 0 to 511, as said below
- counts: int32 [16], P('dp'), may hold values from 1 to 12, 184 in all
- destination: int32 [192, 1], P('dp'), may hold values from 0 to 15; in each aligned block of 12 rows (0 to 11, 12 to 23, ...) no two rows name the same one
Outputs:
- routed: bfloat16 [32768, 4096], P('dp', 'tensor')
Inputs may be any that keep to these rules, and one draw needn't show every extreme that they name: `doc_pos`: 0 at the first row of a document (row 0 and every multiple of 512 are such rows), else one more than on the row before; rows 0 to 511 form one document. `counts`: one device has all its blocks filled. Among the 12 entries of one dp device no destination appears twice.
All inputs are finite; a program needn't handle non-finite values.
Results may differ from a plain program's by a relative error of at most 0.0058.
Values may be sent and summed in bfloat16 or wider, within the bound.
No kernel may reach another device: no remote copies, remote signals or barrier semaphores. Data moves between devices by JAX's collectives and lax.ppermute only.
A program may use at most 128 MiB of HBM per device.

v0:
```python
import jax
import jax.numpy as jnp
from jax import lax
from jax.sharding import PartitionSpec as P

TAPS = 7


def from_behind(block, axis, distance):
    devices = range(lax.axis_size(axis))
    route = [(i - distance, i) for i in devices if i - distance in devices]
    return lax.ppermute(block, axis, route)


def featurize(extended, weights, positions):
    length = positions.shape[0]
    total = jnp.zeros((length, extended.shape[1]), jnp.float32)
    for offset in range(TAPS):
        shifted = extended[TAPS - 1 - offset : TAPS - 1 - offset + length].astype(jnp.float32)
        total = total + jnp.where(
            (positions >= offset)[:, None], weights[offset][None, :] * shifted, 0.0
        )
    return total


def project_terms(mixed, weight_blocks, width, count):
    row_count = mixed.shape[0]
    block_total = count // row_count
    terms = jnp.einsum("rc,cnk->nrk", mixed, weight_blocks, preferred_element_type=jnp.float32)
    return terms.reshape(block_total * row_count, width)


def route_blocks(values, selector, slot_rows):
    flat_blocks = values.reshape(selector.shape[1], -1)
    moved = jnp.dot(selector, flat_blocks, preferred_element_type=jnp.float32).astype(jnp.bfloat16)
    return moved.reshape(selector.shape[0], slot_rows, -1)


def per_device(
    query_in, key_in, value_in, feat_filter, inner_filter, out_weight, doc_pos, counts, destination
):
    row_count, channels = query_in.shape
    tap_reach = TAPS - 1
    history_rows = 2 * tap_reach
    tails = from_behind(
        (
            query_in[row_count - history_rows :],
            key_in[row_count - history_rows :],
            value_in[row_count - history_rows :],
        ),
        "dp",
        1,
    )
    lead_positions = doc_pos[0] - jnp.arange(tap_reach, 0, -1, dtype=jnp.int32)
    wide_positions = jnp.concatenate([lead_positions, doc_pos], axis=0)
    feat_query = featurize(
        jnp.concatenate([tails[0][tap_reach:], query_in], axis=0), feat_filter[0], doc_pos
    )
    feat_key = featurize(
        jnp.concatenate([tails[1], key_in], axis=0), feat_filter[1], wide_positions
    )
    feat_value = featurize(
        jnp.concatenate([tails[2], value_in], axis=0), feat_filter[2], wide_positions
    )
    gated = feat_key * feat_value
    inner = featurize(gated, inner_filter, doc_pos)
    mixed = (feat_query * inner).astype(jnp.bfloat16)
    dp_count = lax.axis_size("dp")
    tp_count = lax.axis_size("tensor")
    block_width = out_weight.shape[1] // tp_count
    weight_blocks = out_weight.reshape(channels, tp_count, block_width)
    block_count = destination.shape[0]
    slot_rows = row_count // block_count
    filled = jnp.arange(block_count, dtype=jnp.int32) < counts[0]
    matches = destination[:, 0][None, :] == jnp.arange(dp_count, dtype=jnp.int32)[:, None]
    selector = (matches & filled[None, :]).astype(jnp.bfloat16)
    summed = lax.psum_scatter(
        project_terms(
            mixed, weight_blocks, block_width, row_count * lax.axis_size("tensor")
        ).astype(jnp.bfloat16),
        "tensor",
        scatter_dimension=0,
        tiled=True,
    )
    moved = lax.all_to_all(
        route_blocks(summed, selector, slot_rows), "dp", split_axis=0, concat_axis=0, tiled=True
    )
    return moved.reshape(dp_count * slot_rows, block_width)


def solution(mesh):
    in_specs = (
        P("dp", "tensor"),
        P("dp", "tensor"),
        P("dp", "tensor"),
        P(None, None, "tensor"),
        P(None, "tensor"),
        P("tensor", None),
        P("dp"),
        P("dp"),
        P("dp", None),
    )
    out_specs = P("dp", "tensor")
    return jax.shard_map(
        per_device, mesh=mesh, in_specs=in_specs, out_specs=out_specs, check_vma=False
    )
```

profile of v0, /device:TPU:16, one launch (start us, length us, event | category | flops | bytes accessed | tf_op | source)
XLA Modules:
  0.0 453.0 jit_solution(6530709098997635421)
XLA Ops:
  6.5 0.9 slice.243
  7.4 3.4 collective-permute-start.1
  10.8 0.9 slice.258
  11.7 3.4 collective-permute-start.2
  15.1 0.9 slice.227
  15.9 3.4 collective-permute-start
  19.3 1.7 fusion.46
  21.1 0.9 fusion.47
  22.0 1.2 slice.241
  23.2 0.7 broadcast_compare_fusion.13
  23.9 0.7 add_subtract_fusion
  24.6 1.2 fusion.48
  25.8 0.8 broadcast_compare_fusion.6
  26.6 0.0 collective-permute-done
  26.7 61.9 %add_multiply_fusion = f32[1542,2048]{1,0:T(8,128)} fusion(bf16[12,2048]{1,0:T(8,128)(2,1)S(1)} %collective-permute-done.2, bf16[12,2048]{1,0:T(8,128)(2,1)S(1)} %collective-permute-done.1, bf16[1536,2048]{1,0:T(8,128)(2,1)} %param.11, bf16[1536,2048]{1,0:T(8,128)(2,1)} %param.10, f32[2048]{0:T(1024)S(1)} %bitcast.84, f32[2048]{0:T(1024)S(1)} %bitcast.83, ...), kind=kLoop, calls=%fused_computation.21 | loop fusion | flops 306327552 | bytes 25438762 | tf_op jit(solution)/shard_map/mul | solution.py:65
  88.6 78.4 %fusion.53 = bf16[1536,2048,1]{1,0,2:T(8,128)(2,1)S(1)} fusion(f32[1542,2048]{1,0:T(8,128)} %add_multiply_fusion, f32[2048]{0:T(1024)S(1)} %bitcast.62, f32[2048]{0:T(1024)S(1)} %bitcast.63, f32[2048]{0:T(1024)S(1)} %bitcast.58, f32[2048]{0:T(1024)S(1)} %bitcast.59, f32[2048]{0:T(1024)S(1)} %bitcast.60, f32[2048]{0:T(1024)S(1)} %bitcast.61, ...), kind=kLoop, calls=%fused_computation.76.clone.1 | loop fusion | flops 210763776 | bytes 100813312 | tf_op jit(solution)/shard_map/rc,cnk->nrk/dot_general | solution.py:29
  167.0 31.3 %fusion.18 = bf16[1536,2,2048]{2,0,1:T(8,128)(2,1)} fusion(bf16[256,2,8,2048]{3,2,1,0:T(8,128)(2,1)} %bitcast.86, bf16[1536,2048,1]{1,0,2:T(8,128)(2,1)S(1)} %fusion.53), kind=kOutput, calls=%fused_computation.44 | convolution fusion | flops 25776095232 | bytes 35651584 | tf_op jit(solution)/shard_map/rc,cnk->nrk/dot_general | solution.py:29
  198.3 0.0 reduce-scatter.2.cloned.1.call-update
  199.0 21.3 %reduce-scatter.2.cloned.1.call-done = bf16[1536,2048]{1,0:T(8,128)(2,1)} async-done(((bf16[3072,2048]{1,0:T(8,128)(2,1)}), bf16[1536,2048]{1,0:T(8,128)(2,1)}) %reduce-scatter.2.cloned.1.call-update) | async-done | bytes 6291472 | tf_op jit(solution)/shard_map/reduce_scatter | solution.py:77
  220.3 8.0 %reshape.161 = bf16[12,262144]{1,0:T(8,128)(2,1)} reshape(bf16[1536,2048]{1,0:T(8,128)(2,1)} %reduce-scatter.2.cloned.1.call-done) | data formatting | bytes 12582912 | tf_op jit(solution)/shard_map/reshape | solution.py:34
  228.3 8.9 %convolution_convert_fusion = bf16[16,262144]{1,0:T(8,128)(2,1)} fusion(bf16[12,262144]{1,0:T(8,128)(2,1)} %reshape.161, s32[12]{0:T(128)S(1)} %bitcast.85, pred[12]{0:T(512)(128)(4,1)S(1)} %iota_compare_fusion.1), kind=kOutput, calls=%fused_computation | convolution fusion | flops 104857984 | bytes 14680124 | tf_op jit(solution)/shard_map/dot_general | solution.py:35
  237.2 11.4 %copy.12 = bf16[2,8,128,2048]{3,2,1,0:T(8,128)(2,1)} copy(bf16[2,8,128,2048]{3,1,2,0:T(8,128)(2,1)} %bitcast.53) | data formatting | bytes 16777216
  248.6 189.1 %all_to_all.5 = bf16[16,128,2048]{2,1,0:T(8,128)(2,1)} all-to-all(bf16[16,128,2048]{2,1,0:T(8,128)(2,1)} %bitcast.54), channel_id=1, replica_groups=mesh['dp'=16,'tensor'=2] {'dp'}, dimensions={0} | all-to-all | bytes 16777216 | tf_op jit(solution)/shard_map/all_to_all | solution.py:85
  437.7 8.4 %copy.22 = bf16[2048,2048]{1,0:T(8,128)(2,1)} copy(bf16[2048,2048]{1,0:T(8,128)(2,1)} %bitcast.55) | data formatting | bytes 16777216
  (7 shorter events, 0.0 us)
Async XLA Ops:
  6.5 213.7 %reduce-scatter.2.cloned.1.call-start = ((), (), s32[]{:S(2)}) async-start(), calls=%async_computation.2 | async-start | bytes 18874368 | tf_op jit(solution)/shard_map/reduce_scatter | solution.py:77
  7.4 19.3 %collective-permute-start.1 = (bf16[12,2048]{1,0:T(8,128)(2,1)S(1)}, bf16[12,2048]{1,0:T(8,128)(2,1)S(1)}, u32[]{:S(2)}, u32[]{:S(2)}) collective-permute-start(bf16[12,2048]{1,0:T(8,128)(2,1)S(1)} %slice.243), channel_id=1, source_target_pairs={{0,2},{2,4},{4,6},{6,8},{8,10},{10,12},{12,14},{14,16},{16,18},{18... | collective-permute-start | bytes 147464 | tf_op jit(solution)/shard_map/ppermute | solution.py:12
  11.7 15.0 %collective-permute-start.2 = (bf16[12,2048]{1,0:T(8,128)(2,1)S(1)}, bf16[12,2048]{1,0:T(8,128)(2,1)S(1)}, u32[]{:S(2)}, u32[]{:S(2)}) collective-permute-start(bf16[12,2048]{1,0:T(8,128)(2,1)S(1)} %slice.258), channel_id=1, source_target_pairs={{0,2},{2,4},{4,6},{6,8},{8,10},{10,12},{12,14},{14,16},{16,18},{18... | collective-permute-start | bytes 147464 | tf_op jit(solution)/shard_map/ppermute | solution.py:12
  15.9 10.7 %collective-permute-start = (bf16[12,2048]{1,0:T(8,128)(2,1)S(1)}, bf16[12,2048]{1,0:T(8,128)(2,1)S(1)}, u32[]{:S(2)}, u32[]{:S(2)}) collective-permute-start(bf16[12,2048]{1,0:T(8,128)(2,1)S(1)} %slice.227), channel_id=1, source_target_pairs={{0,2},{2,4},{4,6},{6,8},{8,10},{10,12},{12,14},{14,16},{16,18},{18... | collective-permute-start | bytes 147464 | tf_op jit(solution)/shard_map/ppermute | solution.py:12
  198.3 30.0 %copy-start = (s32[12,1]{0,1:T(1,128)S(1)}, s32[12,1]{0,1:T(1,128)}, u32[]{:S(2)}) copy-start(s32[12,1]{0,1:T(1,128)} %param.17) | copy-start | bytes 148
Sparse Core Ops, SparseCore 0:
  198.5 21.7 reduce-scatter.1
where the time goes:
time: 457 us; the launch traced here: 453 us
  blocking collectives  189 us (41%)
  other arithmetic  142 us (31%)
  matrix products  40.3 us (9%)
  local copies, waits for them, and re-layouts  35.6 us (8%)
  waiting for transfers between devices  21.3 us (5%)
  between operations  14.1 us (3%)
  starting transfers between devices  10.2 us (2%)
    all_to_all x1, blocking collectives, per_device(): lax.all_to_all(route_blocks(summed, selector, slot_rows), 'dp', split_axi...  189 us
    dot_general x1, other arithmetic, project_terms(): jnp.einsum('rc,cnk->nrk', mixed, weight_blocks, preferred_element_type=jn...  78.4 us
    mul x1, other arithmetic, per_device(): gated = feat_key * feat_value  61.9 us
    dot_general x1, matrix products, project_terms(): jnp.einsum('rc,cnk->nrk', mixed, weight_blocks, preferred_element_type=jn...  31.3 us
    reduce_scatter x1, waiting for transfers between devices, per_device(): lax.psum_scatter(project_terms(mixed, weight_blocks, block_width, row_cou...  21.3 us
    unnamed x4, local copies, waits for them, and re-layouts  19.9 us
    ppermute x3, starting transfers between devices, from_behind(): return lax.ppermute(block, axis, route)  10.2 us
  transfers between devices with their start and end apart: 4, of which 1 were waited for; matrix products, arithmetic and copies ran while one was open for 2% of the time, Pallas kernels for 0%

commit v1 on v0

v1 whole, which is shorter than its diff:
```python
import functools

import jax
import jax.numpy as jnp
from jax import lax
from jax.experimental import pallas as pl
from jax.experimental.pallas import tpu as pltpu
from jax.sharding import PartitionSpec as P

TAPS = 7
LEAD = 16
TILE = 32
LANES = 128


def taps_sum(ref, start, rows, weights, positions):
    total = None
    for offset in range(TAPS):
        term = weights[offset] * ref[start - offset : start - offset + rows, :]
        if positions is not None:
            term = jnp.where(positions >= offset, term, 0.0)
        total = term if total is None else total + term
    return total


def mix_kernel(
    slots, parts, width,
    block_of, clean, lead_clean, core,
    q_ref, k_ref, v_ref, qp_ref, kp_ref, vp_ref, tails_ref, pos_ref, feat_ref, inner_ref, w_hbm,
    *rest,
):
    outs, (qx, kx, vx, gx, mixed, w_ref, sem) = rest[:-7], rest[-7:]
    slot = pl.program_id(0)
    block_rows, channels = q_ref.shape
    tiles = block_rows // TILE
    w_copy = pltpu.make_async_copy(w_hbm, w_ref, sem)

    @pl.when(slot == 0)
    def _():
        w_copy.start()

    block = block_of[slot]
    base = pl.multiple_of(slot * block_rows, block_rows)

    @pl.when(block < 0)
    def _():
        mixed[pl.ds(base, block_rows), :] = jnp.zeros((block_rows, channels), mixed.dtype)

    @pl.when(block >= 0)
    def _():
        def one_chunk(c, carry):
            lanes = pl.ds(pl.multiple_of(c * LANES, LANES), LANES)
            for i, (dst, src, before) in enumerate(
                ((qx, q_ref, qp_ref), (kx, k_ref, kp_ref), (vx, v_ref, vp_ref))
            ):
                dst[LEAD:, :] = src[:, lanes].astype(jnp.float32)

                @pl.when(block == 0)
                def _():
                    dst[:LEAD, :] = tails_ref[i, :, lanes].astype(jnp.float32)

                @pl.when(block > 0)
                def _():
                    dst[:LEAD, :] = before[:, lanes].astype(jnp.float32)

            feat = [[feat_ref[i, t : t + 1, lanes] for t in range(TAPS)] for i in range(3)]
            inner = [inner_ref[t : t + 1, lanes] for t in range(TAPS)]

            def lead(masked):
                rows = 8
                positions = None
                if masked:
                    positions = pos_ref[0:1, :] - (
                        rows - lax.broadcasted_iota(jnp.int32, (rows, LANES), 0)
                    )
                gx[0:rows, :] = taps_sum(kx, LEAD - rows, rows, feat[1], positions) * taps_sum(
                    vx, LEAD - rows, rows, feat[2], positions
                )

            @pl.when(lead_clean[block] > 0)
            def _():
                lead(False)

            @pl.when(lead_clean[block] == 0)
            def _():
                lead(True)

            def tile_of(t, masked):
                first = t * TILE
                positions = pos_ref[first : first + TILE, :] if masked else None
                gx[8 + first : 8 + first + TILE, :] = taps_sum(
                    kx, LEAD + first, TILE, feat[1], positions
                ) * taps_sum(vx, LEAD + first, TILE, feat[2], positions)
                query = taps_sum(qx, LEAD + first, TILE, feat[0], positions)
                result = query * taps_sum(gx, 8 + first, TILE, inner, positions)
                mixed[pl.ds(pl.multiple_of(base + first, TILE), TILE), lanes] = result.astype(
                    mixed.dtype
                )

            for t in range(tiles):
                flag = clean[block * tiles + t]

                @pl.when(flag > 0)
                def _():
                    tile_of(t, False)

                @pl.when(flag == 0)
                def _():
                    tile_of(t, True)

            return carry

        lax.fori_loop(0, channels // LANES, one_chunk, 0)

    @pl.when(slot == slots - 1)
    def _():
        w_copy.wait()
        step = min(width, 512)
        for j in range(parts):
            first = lax.rem(core[0] + j, parts) * width if len(outs) > 1 else j * width

            def columns(n, carry):
                at = pl.multiple_of(first + n * step, step)
                part = jnp.dot(
                    mixed[...], w_ref[:, pl.ds(at, step)], preferred_element_type=jnp.float32
                ).astype(jnp.bfloat16)
                to = pl.ds(pl.multiple_of(n * step, step), step)
                if len(outs) > 1:
                    for s in range(slots):
                        outs[j][s, :, to] = part[s * block_rows : (s + 1) * block_rows]
                else:
                    outs[0][j, :, to] = part
                return carry

            lax.fori_loop(0, width // step, columns, 0)


def mix_blocks(scalars, streams, tails, positions, feat_filter, inner_filter, out_weight, parts, block_rows):
    slots = scalars[0].shape[0]
    rows, channels = streams[0].shape
    width = out_weight.shape[1] // parts
    lead_per_block = block_rows // LEAD

    def here(s, block_of, *_):
        return (jnp.maximum(block_of[s], 0), 0)

    def before(s, block_of, *_):
        return (jnp.maximum(block_of[s] * lead_per_block - 1, 0), 0)

    whole = lambda shape: pl.BlockSpec(shape, lambda *_: (0,) * len(shape))
    pair = parts == 2
    if pair:
        shapes = [jax.ShapeDtypeStruct((slots, block_rows, width), jnp.bfloat16)] * 2
    else:
        shapes = [jax.ShapeDtypeStruct((parts, slots * block_rows, width), jnp.bfloat16)]
    filled_flops = 2 * slots * block_rows * channels * out_weight.shape[1]
    return pl.pallas_call(
        functools.partial(mix_kernel, slots, parts, width),
        out_shape=shapes,
        grid_spec=pltpu.PrefetchScalarGridSpec(
            num_scalar_prefetch=4,
            grid=(slots,),
            in_specs=[pl.BlockSpec((block_rows, channels), here)] * 3
            + [pl.BlockSpec((LEAD, channels), before)] * 3
            + [
                whole(tails.shape),
                pl.BlockSpec((block_rows, LANES), here),
                whole(feat_filter.shape),
                whole(inner_filter.shape),
                pl.BlockSpec(memory_space=pl.ANY),
            ],
            out_specs=[whole(s.shape) for s in shapes],
            scratch_shapes=[pltpu.VMEM((LEAD + block_rows, LANES), jnp.float32)] * 3
            + [
                pltpu.VMEM((8 + block_rows, LANES), jnp.float32),
                pltpu.VMEM((slots * block_rows, channels), jnp.bfloat16),
                pltpu.VMEM(out_weight.shape, out_weight.dtype),
                pltpu.SemaphoreType.DMA,
            ],
        ),
        compiler_params=pltpu.CompilerParams(
            vmem_limit_bytes=48 * 1024 * 1024, dimension_semantics=("arbitrary",)
        ),
        cost_estimate=pl.CostEstimate(
            flops=filled_flops, bytes_accessed=16 * 1024 * 1024 + slots * 6 * 1024 * 1024, transcendentals=0
        ),
    )(*scalars, *streams, *streams, tails, positions, feat_filter, inner_filter, out_weight)


def per_device(
    query_in, key_in, value_in, feat_filter, inner_filter, out_weight, doc_pos, counts, destination
):
    row_count, channels = query_in.shape
    dp_count = lax.axis_size("dp")
    tp_count = lax.axis_size("tensor")
    me = lax.axis_index("dp")
    core = lax.axis_index("tensor").astype(jnp.int32).reshape(1)
    block_count = destination.shape[0]
    block_rows = row_count // block_count
    width = out_weight.shape[1] // tp_count
    streams = (query_in, key_in, value_in)

    tails = lax.ppermute(
        jnp.stack([x[row_count - LEAD :] for x in streams]),
        "dp",
        [(i, i + 1) for i in range(dp_count - 1)],
    )
    positions = jnp.broadcast_to(doc_pos[:, None], (row_count, LANES))
    clean = (jnp.min(doc_pos.reshape(-1, TILE), axis=1) >= TAPS - 1).astype(jnp.int32)
    lead_clean = (doc_pos.reshape(block_count, block_rows)[:, 0] >= 2 * (TAPS - 1)).astype(jnp.int32)

    half = dp_count // 2
    order = [r for pair in zip(range(half, dp_count), list(range(1, half)) + [0]) for r in pair]
    partner = jnp.bitwise_xor(me.astype(jnp.int32), jnp.asarray(order, jnp.int32))
    numbers = jnp.arange(block_count, dtype=jnp.int32)
    named = (destination[:, 0][None, :] == partner[:, None]) & (numbers < counts[0])[None, :]
    block_of = jnp.max(jnp.where(named, numbers[None, :], -1), axis=1)

    result = jnp.zeros((dp_count, block_rows, width), jnp.bfloat16)
    group = 2
    for first in range(0, dp_count, group):
        terms = mix_blocks(
            (block_of[first : first + group], clean, lead_clean, core),
            streams, tails, positions, feat_filter, inner_filter, out_weight, tp_count, block_rows,
        )
        if tp_count == 2:
            other = lax.ppermute(terms[1], "tensor", [(0, 1), (1, 0)])
        else:
            summed = lax.psum_scatter(terms[0], "tensor", scatter_dimension=0, tiled=False)
            summed = summed.reshape(group, block_rows, width)
        for s in range(group):
            r = order[first + s]
            if tp_count == 2:
                block = (
                    terms[0][s].astype(jnp.float32) + other[s].astype(jnp.float32)
                ).astype(jnp.bfloat16)
            else:
                block = summed[s]
            if r:
                block = lax.ppermute(block, "dp", [(i, i ^ r) for i in range(dp_count)])
            result = lax.dynamic_update_index_in_dim(result, block, jnp.bitwise_xor(me, r), 0)
    return result.reshape(dp_count * block_rows, width)


def solution(mesh):
    in_specs = (
        P("dp", "tensor"),
        P("dp", "tensor"),
        P("dp", "tensor"),
        P(None, None, "tensor"),
        P(None, "tensor"),
        P("tensor", None),
        P("dp"),
        P("dp"),
        P("dp", None),
    )
    return jax.shard_map(
        per_device, mesh=mesh, in_specs=in_specs, out_specs=P("dp", "tensor"), check_vma=False
    )
```

time: 457 us -> 349 us (0.76)
  blocking collectives: 189 us -> 0 us
  other arithmetic: 142 us -> 12.9 us
  waiting for transfers between devices: 21.3 us -> 150 us
  Pallas kernels: 0 us -> 124 us
  matrix products: 40.3 us -> 0 us
  starting transfers between devices: 10.2 us -> 47.3 us
  local copies, waits for them, and re-layouts: 35.6 us -> 10.5 us
  between operations: 14.1 us -> 1.22 us
    all_to_all x1 -> x0, blocking collectives: 189 us -> none  [per_device(): lax.all_to_all(route_blocks(summed, selector, slot_rows), 'dp', split_axi...]
    ppermute x3 -> x24, waiting for transfers between devices: 0.01 us -> 150 us  [the longest x15 147 us: per_device(): block = lax.ppermute(block, 'dp', [(i, i ^ r) for i in range(dp_count)])]
    pallas_call x0 -> x8, Pallas kernels: none -> 124 us  [mix_blocks(): pl.pallas_call(functools.partial(mix_kernel, slots, parts, width), out_sh...]
    dot_general x1 -> x0, other arithmetic: 78.4 us -> none  [project_terms(): jnp.einsum('rc,cnk->nrk', mixed, weight_blocks, preferred_element_type=jn...]
    mul x1 -> x0, other arithmetic: 61.9 us -> none  [per_device(): gated = feat_key * feat_value]
    dot_general x2 -> x0, matrix products: 40.3 us -> none  [the longest x1 31.3 us: project_terms(): jnp.einsum('rc,cnk->nrk', mixed, weight_blocks, preferred_element_type=jn...]
    ppermute x3 -> x24, starting transfers between devices: 10.2 us -> 47.3 us  [the longest x15 41.5 us: per_device(): block = lax.ppermute(block, 'dp', [(i, i ^ r) for i in range(dp_count)])]
    reduce_scatter x1 -> x0, waiting for transfers between devices: 21.3 us -> none  [per_device(): lax.psum_scatter(project_terms(mixed, weight_blocks, block_width, row_cou...]
  transfers between devices with their start and end apart: 4 -> 24, of which waited for: 1 -> 12; matrix products, arithmetic and copies ran while one was open for 2% -> 4% of each run, Pallas kernels for 0% -> 31%
where the time goes in v1:
time: 349 us; the launch traced here: 345 us
  waiting for transfers between devices  150 us (43%)
  Pallas kernels  124 us (36%)
  starting transfers between devices  47.3 us (14%)
  other arithmetic  12.9 us (4%)
  local copies, waits for them, and re-layouts  10.5 us (3%)
    ppermute x15, waiting for transfers between devices, per_device(): block = lax.ppermute(block, 'dp', [(i, i ^ r) for i in range(dp_count)])  147 us
    pallas_call x8, Pallas kernels, mix_blocks(): pl.pallas_call(functools.partial(mix_kernel, slots, parts, width), out_sh...  124 us
    ppermute x15, starting transfers between devices, per_device(): block = lax.ppermute(block, 'dp', [(i, i ^ r) for i in range(dp_count)])  41.5 us
    convert_element_type x8, other arithmetic, per_device(): block = (terms[0][s].astype(jnp.float32) + other[s].astype(jnp.float32))....  10.3 us
  transfers between devices with their start and end apart: 24, of which 12 were waited for; matrix products, arithmetic and copies ran while one was open for 4% of the time, Pallas kernels for 31%

profile of v1, /device:TPU:16, one launch (start us, length us, event | category | flops | bytes accessed | tf_op | source)
XLA Modules:
  0.0 345.4 jit_solution(8200483297304099958)
XLA Ops:
  1.8 3.4 collective-permute-start
  9.3 2.8 collective-permute-done.tails_ref
  14.8 17.4 %shard_map.100 = (bf16[2,128,2048]{2,1,0:T(8,128)(2,1)S(1)}, bf16[2,128,2048]{2,1,0:T(8,128)(2,1)}) custom-call(s32[2]{0:T(128)S(1)} %get-tuple-element.58.block_of, s32[48]{0:T(128)S(1)} %compare_convert_fusion.clean, s32[12]{0:T(128)S(1)} %convert_reduce_fusion.lead_clean, s32[1]{0:T(128)} %bitcast.3.core, bf16[1536,2048]{1,0:T(8,128)(2,1)} %qp_ref.15, ...), custom_call_target="tpu_custom_call" | custom-call | flops 4294967296 | bytes 29360128 | tf_op jit(solution)/shard_map/pallas_call | solution.py:157
  32.3 14.7 %shard_map.101 = (bf16[2,128,2048]{2,1,0:T(8,128)(2,1)S(1)}, bf16[2,128,2048]{2,1,0:T(8,128)(2,1)}) custom-call(s32[2]{0:T(128)S(1)} %get-tuple-element.57.block_of, s32[48]{0:T(128)S(1)} %compare_convert_fusion.clean, s32[12]{0:T(128)S(1)} %convert_reduce_fusion.lead_clean, s32[1]{0:T(128)} %bitcast.3.core, bf16[1536,2048]{1,0:T(8,128)(2,1)} %qp_ref.15, ...), custom_call_target="tpu_custom_call" | custom-call | flops 4294967296 | bytes 29360128 | tf_op jit(solution)/shard_map/pallas_call | solution.py:157
  47.6 17.0 %shard_map.102 = (bf16[2,128,2048]{2,1,0:T(8,128)(2,1)S(1)}, bf16[2,128,2048]{2,1,0:T(8,128)(2,1)}) custom-call(s32[2]{0:T(128)S(1)} %get-tuple-element.56.block_of, s32[48]{0:T(128)S(1)} %compare_convert_fusion.clean, s32[12]{0:T(128)S(1)} %convert_reduce_fusion.lead_clean, s32[1]{0:T(128)} %bitcast.3.core, bf16[1536,2048]{1,0:T(8,128)(2,1)} %qp_ref.15, ...), custom_call_target="tpu_custom_call" | custom-call | flops 4294967296 | bytes 29360128 | tf_op jit(solution)/shard_map/pallas_call | solution.py:157
  64.7 16.2 %shard_map.103 = (bf16[2,128,2048]{2,1,0:T(8,128)(2,1)S(1)}, bf16[2,128,2048]{2,1,0:T(8,128)(2,1)S(1)}) custom-call(s32[2]{0:T(128)S(1)} %get-tuple-element.55.block_of, s32[48]{0:T(128)S(1)} %compare_convert_fusion.clean, s32[12]{0:T(128)S(1)} %convert_reduce_fusion.lead_clean, s32[1]{0:T(128)} %bitcast.3.core, bf16[1536,2048]{1,0:T(8,128)(2,1)} %qp_ref.15, ...), custom_call_target="tpu_custom_call" | custom-call | flops 4294967296 | bytes 29360128 | tf_op jit(solution)/shard_map/pallas_call | solution.py:157
  81.4 16.5 %shard_map.104 = (bf16[2,128,2048]{2,1,0:T(8,128)(2,1)S(1)}, bf16[2,128,2048]{2,1,0:T(8,128)(2,1)S(1)}) custom-call(s32[2]{0:T(128)S(1)} %get-tuple-element.54.block_of, s32[48]{0:T(128)S(1)} %compare_convert_fusion.clean, s32[12]{0:T(128)S(1)} %convert_reduce_fusion.lead_clean, s32[1]{0:T(128)} %bitcast.3.core, bf16[1536,2048]{1,0:T(8,128)(2,1)} %qp_ref.15, ...), custom_call_target="tpu_custom_call" | custom-call | flops 4294967296 | bytes 29360128 | tf_op jit(solution)/shard_map/pallas_call | solution.py:157
  98.1 13.8 %shard_map.105 = (bf16[2,128,2048]{2,1,0:T(8,128)(2,1)S(1)}, bf16[2,128,2048]{2,1,0:T(8,128)(2,1)S(1)}) custom-call(s32[2]{0:T(128)S(1)} %get-tuple-element.53.block_of, s32[48]{0:T(128)S(1)} %compare_convert_fusion.clean, s32[12]{0:T(128)S(1)} %convert_reduce_fusion.lead_clean, s32[1]{0:T(128)} %bitcast.3.core, bf16[1536,2048]{1,0:T(8,128)(2,1)} %qp_ref.15, ...), custom_call_target="tpu_custom_call" | custom-call | flops 4294967296 | bytes 29360128 | tf_op jit(solution)/shard_map/pallas_call | solution.py:157
  111.8 14.2 %shard_map.106 = (bf16[2,128,2048]{2,1,0:T(8,128)(2,1)S(1)}, bf16[2,128,2048]{2,1,0:T(8,128)(2,1)S(1)}) custom-call(s32[2]{0:T(128)S(1)} %get-tuple-element.52.block_of, s32[48]{0:T(128)S(1)} %compare_convert_fusion.clean, s32[12]{0:T(128)S(1)} %convert_reduce_fusion.lead_clean, s32[1]{0:T(128)} %bitcast.3.core, bf16[1536,2048]{1,0:T(8,128)(2,1)} %qp_ref.15, ...), custom_call_target="tpu_custom_call" | custom-call | flops 4294967296 | bytes 29360128 | tf_op jit(solution)/shard_map/pallas_call | solution.py:157
  126.1 14.0 %shard_map.107 = (bf16[2,128,2048]{2,1,0:T(8,128)(2,1)S(1)}, bf16[2,128,2048]{2,1,0:T(8,128)(2,1)S(1)}) custom-call(s32[2]{0:T(128)S(1)} %get-tuple-element.51.block_of, s32[48]{0:T(128)S(1)} %compare_convert_fusion.clean, s32[12]{0:T(128)S(1)} %convert_reduce_fusion.lead_clean, s32[1]{0:T(128)} %bitcast.3.core, bf16[1536,2048]{1,0:T(8,128)(2,1)} %qp_ref.15, ...), custom_call_target="tpu_custom_call" | custom-call | flops 4294967296 | bytes 29360128 | tf_op jit(solution)/shard_map/pallas_call | solution.py:157
  149.0 3.5 %collective-permute-start.3 = (bf16[128,2048]{1,0:T(8,128)(2,1)S(1)}, bf16[128,2048]{1,0:T(8,128)(2,1)S(1)}, u32[]{:S(2)}, u32[]{:S(2)}) collective-permute-start(bf16[128,2048]{1,0:T(8,128)(2,1)S(1)} %get-tuple-element.49), channel_id=1, source_target_pairs={{0,2},{2,0},{4,6},{6,4},{8,10},{10,8},{12,14},{14,12},{16,18},{18,... | collective-permute-start | bytes 1572872 | tf_op jit(solution)/shard_map/ppermute | solution.py:240
  159.6 33.7 %collective-permute-done.2 = bf16[128,2048]{1,0:T(8,128)(2,1)S(1)} collective-permute-done((bf16[128,2048]{1,0:T(8,128)(2,1)S(1)}, bf16[128,2048]{1,0:T(8,128)(2,1)S(1)}, u32[]{:S(2)}, u32[]{:S(2)}) %collective-permute-start.2) | collective-permute-done | bytes 524320 | tf_op jit(solution)/shard_map/ppermute | solution.py:240
  194.5 5.8 %collective-permute-start.11 = (bf16[128,2048]{1,0:T(8,128)(2,1)S(1)}, bf16[128,2048]{1,0:T(8,128)(2,1)S(1)}, u32[]{:S(2)}, u32[]{:S(2)}) collective-permute-start(bf16[128,2048]{1,0:T(8,128)(2,1)S(1)} %get-tuple-element.44), channel_id=1, source_target_pairs={{0,22},{2,20},{4,18},{6,16},{8,30},{10,28},{12,26},{14,24},{16,6},... | collective-permute-start | bytes 1572872 | tf_op jit(solution)/shard_map/ppermute | solution.py:240
  200.4 15.5 %collective-permute-done.5 = bf16[128,2048]{1,0:T(8,128)(2,1)S(1)} collective-permute-done((bf16[128,2048]{1,0:T(8,128)(2,1)S(1)}, bf16[128,2048]{1,0:T(8,128)(2,1)S(1)}, u32[]{:S(2)}, u32[]{:S(2)}) %collective-permute-start.5) | collective-permute-done | bytes 524320 | tf_op jit(solution)/shard_map/ppermute | solution.py:240
  220.3 7.4 %collective-permute-done.8 = bf16[128,2048]{1,0:T(8,128)(2,1)S(1)} collective-permute-done((bf16[128,2048]{1,0:T(8,128)(2,1)}, bf16[128,2048]{1,0:T(8,128)(2,1)S(1)}, u32[]{:S(2)}, u32[]{:S(2)}) %collective-permute-start.8) | collective-permute-done | bytes 524320 | tf_op jit(solution)/shard_map/ppermute | solution.py:240
  228.1 16.1 %collective-permute-start.17 = (bf16[128,2048]{1,0:T(8,128)(2,1)S(1)}, bf16[128,2048]{1,0:T(8,128)(2,1)S(1)}, u32[]{:S(2)}, u32[]{:S(2)}) collective-permute-start(bf16[128,2048]{1,0:T(8,128)(2,1)S(1)} %get-tuple-element.40), channel_id=1, source_target_pairs={{0,26},{2,24},{4,30},{6,28},{8,18},{10,16},{12,22},{14,20},{16,10}... | collective-permute-start | bytes 1572872 | tf_op jit(solution)/shard_map/ppermute | solution.py:240
  244.2 5.4 %collective-permute-done.11 = bf16[128,2048]{1,0:T(8,128)(2,1)S(1)} collective-permute-done((bf16[128,2048]{1,0:T(8,128)(2,1)S(1)}, bf16[128,2048]{1,0:T(8,128)(2,1)S(1)}, u32[]{:S(2)}, u32[]{:S(2)}) %collective-permute-start.11) | collective-permute-done | bytes 524320 | tf_op jit(solution)/shard_map/ppermute | solution.py:240
  249.6 3.1 collective-permute-start.18
  252.7 20.9 %collective-permute-done.12 = bf16[128,2048]{1,0:T(8,128)(2,1)S(1)} collective-permute-done((bf16[128,2048]{1,0:T(8,128)(2,1)S(1)}, bf16[128,2048]{1,0:T(8,128)(2,1)S(1)}, u32[]{:S(2)}, u32[]{:S(2)}) %collective-permute-start.12) | collective-permute-done | bytes 524320 | tf_op jit(solution)/shard_map/ppermute | solution.py:240
  278.3 17.7 %collective-permute-done.15 = bf16[128,2048]{1,0:T(8,128)(2,1)S(1)} collective-permute-done((bf16[128,2048]{1,0:T(8,128)(2,1)S(1)}, bf16[128,2048]{1,0:T(8,128)(2,1)S(1)}, u32[]{:S(2)}, u32[]{:S(2)}) %collective-permute-start.15) | collective-permute-done | bytes 524320 | tf_op jit(solution)/shard_map/ppermute | solution.py:240
  297.7 23.4 %collective-permute-done.18 = bf16[128,2048]{1,0:T(8,128)(2,1)S(1)} collective-permute-done((bf16[128,2048]{1,0:T(8,128)(2,1)S(1)}, bf16[128,2048]{1,0:T(8,128)(2,1)S(1)}, u32[]{:S(2)}, u32[]{:S(2)}) %collective-permute-start.18) | collective-permute-done | bytes 524320 | tf_op jit(solution)/shard_map/ppermute | solution.py:240
  321.2 17.8 %collective-permute-done.20 = bf16[128,2048]{1,0:T(8,128)(2,1)S(1)} collective-permute-done((bf16[128,2048]{1,0:T(8,128)(2,1)S(1)}, bf16[128,2048]{1,0:T(8,128)(2,1)S(1)}, u32[]{:S(2)}, u32[]{:S(2)}) %collective-permute-start.20) | collective-permute-done | bytes 524320 | tf_op jit(solution)/shard_map/ppermute | solution.py:240
  339.2 2.6 collective-permute-done.23
  342.0 3.4 copy-done.2
  (75 shorter events, 38.0 us)
Async XLA Ops:
  1.8 10.3 %collective-permute-start = (bf16[3,16,2048]{2,1,0:T(8,128)(2,1)S(1)}, bf16[3,16,2048]{2,1,0:T(8,128)(2,1)S(1)}, u32[]{:S(2)}, u32[]{:S(2)}) collective-permute-start(bf16[3,16,2048]{2,1,0:T(8,128)(2,1)S(1)} %pad_maximum_fusion), channel_id=1, source_target_pairs={{0,2},{2,4},{4,6},{6,8},{8,10},{10,12},{12,14},{14,16},{16,18},{18... | collective-permute-start | bytes 589832 | tf_op jit(solution)/shard_map/ppermute | solution.py:203
  32.2 107.8 %collective-permute-start.1 = (bf16[2,128,2048]{2,1,0:T(8,128)(2,1)}, bf16[2,128,2048]{2,1,0:T(8,128)(2,1)}, u32[]{:S(2)}, u32[]{:S(2)}) collective-permute-start(bf16[2,128,2048]{2,1,0:T(8,128)(2,1)} %get-tuple-element.22), channel_id=1, source_target_pairs={{0,1},{1,0},{2,3},{3,2},{4,5},{5,4},{6,7},{7,6},{8,9},{9,8},{10,11... | collective-permute-start | bytes 3145736 | tf_op jit(solution)/shard_map/ppermute | solution.py:227
  47.0 95.1 %collective-permute-start.4 = (bf16[2,128,2048]{2,1,0:T(8,128)(2,1)}, bf16[2,128,2048]{2,1,0:T(8,128)(2,1)}, u32[]{:S(2)}, u32[]{:S(2)}) collective-permute-start(bf16[2,128,2048]{2,1,0:T(8,128)(2,1)} %get-tuple-element.24), channel_id=1, source_target_pairs={{0,1},{1,0},{2,3},{3,2},{4,5},{5,4},{6,7},{7,6},{8,9},{9,8},{10,11... | collective-permute-start | bytes 3145736 | tf_op jit(solution)/shard_map/ppermute | solution.py:227
  64.6 80.0 %collective-permute-start.7 = (bf16[2,128,2048]{2,1,0:T(8,128)(2,1)}, bf16[2,128,2048]{2,1,0:T(8,128)(2,1)}, u32[]{:S(2)}, u32[]{:S(2)}) collective-permute-start(bf16[2,128,2048]{2,1,0:T(8,128)(2,1)} %get-tuple-element.26), channel_id=1, source_target_pairs={{0,1},{1,0},{2,3},{3,2},{4,5},{5,4},{6,7},{7,6},{8,9},{9,8},{10,11... | collective-permute-start | bytes 3145736 | tf_op jit(solution)/shard_map/ppermute | solution.py:227
  80.9 66.5 %collective-permute-start.10 = (bf16[2,128,2048]{2,1,0:T(8,128)(2,1)S(1)}, bf16[2,128,2048]{2,1,0:T(8,128)(2,1)}, u32[]{:S(2)}, u32[]{:S(2)}) collective-permute-start(bf16[2,128,2048]{2,1,0:T(8,128)(2,1)S(1)} %get-tuple-element.28), channel_id=1, source_target_pairs={{0,1},{1,0},{2,3},{3,2},{4,5},{5,4},{6,7},{7,6},{8,9},{9,8},{10,11... | collective-permute-start | bytes 3145736 | tf_op jit(solution)/shard_map/ppermute | solution.py:227
  98.0 51.0 %collective-permute-start.13 = (bf16[2,128,2048]{2,1,0:T(8,128)(2,1)S(1)}, bf16[2,128,2048]{2,1,0:T(8,128)(2,1)}, u32[]{:S(2)}, u32[]{:S(2)}) collective-permute-start(bf16[2,128,2048]{2,1,0:T(8,128)(2,1)S(1)} %get-tuple-element.30), channel_id=1, source_target_pairs={{0,1},{1,0},{2,3},{3,2},{4,5},{5,4},{6,7},{7,6},{8,9},{9,8},{10,11... | collective-permute-start | bytes 3145736 | tf_op jit(solution)/shard_map/ppermute | solution.py:227
  140.0 14.1 %collective-permute-start.16 = (bf16[2,128,2048]{2,1,0:T(8,128)(2,1)S(1)}, bf16[2,128,2048]{2,1,0:T(8,128)(2,1)S(1)}, u32[]{:S(2)}, u32[]{:S(2)}) collective-permute-start(bf16[2,128,2048]{2,1,0:T(8,128)(2,1)S(1)} %get-tuple-element.32), channel_id=1, source_target_pairs={{0,1},{1,0},{2,3},{3,2},{4,5},{5,4},{6,7},{7,6},{8,9},{9,8},{10,11... | collective-permute-start | bytes 3145736 | tf_op jit(solution)/shard_map/ppermute | solution.py:227
  142.1 14.8 %collective-permute-start.19 = (bf16[2,128,2048]{2,1,0:T(8,128)(2,1)S(1)}, bf16[2,128,2048]{2,1,0:T(8,128)(2,1)S(1)}, u32[]{:S(2)}, u32[]{:S(2)}) collective-permute-start(bf16[2,128,2048]{2,1,0:T(8,128)(2,1)S(1)} %get-tuple-element.34), channel_id=1, source_target_pairs={{0,1},{1,0},{2,3},{3,2},{4,5},{5,4},{6,7},{7,6},{8,9},{9,8},{10,11... | collective-permute-start | bytes 3145736 | tf_op jit(solution)/shard_map/ppermute | solution.py:227
  144.6 12.8 %collective-permute-start.22 = (bf16[2,128,2048]{2,1,0:T(8,128)(2,1)S(1)}, bf16[2,128,2048]{2,1,0:T(8,128)(2,1)S(1)}, u32[]{:S(2)}, u32[]{:S(2)}) collective-permute-start(bf16[2,128,2048]{2,1,0:T(8,128)(2,1)S(1)} %get-tuple-element.36), channel_id=1, source_target_pairs={{0,1},{1,0},{2,3},{3,2},{4,5},{5,4},{6,7},{7,6},{8,9},{9,8},{10,11... | collective-permute-start | bytes 3145736 | tf_op jit(solution)/shard_map/ppermute | solution.py:227
  147.4 46.0 %collective-permute-start.2 = (bf16[128,2048]{1,0:T(8,128)(2,1)S(1)}, bf16[128,2048]{1,0:T(8,128)(2,1)S(1)}, u32[]{:S(2)}, u32[]{:S(2)}) collective-permute-start(bf16[128,2048]{1,0:T(8,128)(2,1)S(1)} %get-tuple-element.50), channel_id=1, source_target_pairs={{0,16},{2,18},{4,20},{6,22},{8,24},{10,26},{12,28},{14,30},{16,0},... | collective-permute-start | bytes 1572872 | tf_op jit(solution)/shard_map/ppermute | solution.py:240
  149.0 45.5 %collective-permute-start.3 = (bf16[128,2048]{1,0:T(8,128)(2,1)S(1)}, bf16[128,2048]{1,0:T(8,128)(2,1)S(1)}, u32[]{:S(2)}, u32[]{:S(2)}) collective-permute-start(bf16[128,2048]{1,0:T(8,128)(2,1)S(1)} %get-tuple-element.49), channel_id=1, source_target_pairs={{0,2},{2,0},{4,6},{6,4},{8,10},{10,8},{12,14},{14,12},{16,18},{18,... | collective-permute-start | bytes 1572872 | tf_op jit(solution)/shard_map/ppermute | solution.py:240
  154.1 61.7 %collective-permute-start.5 = (bf16[128,2048]{1,0:T(8,128)(2,1)S(1)}, bf16[128,2048]{1,0:T(8,128)(2,1)S(1)}, u32[]{:S(2)}, u32[]{:S(2)}) collective-permute-start(bf16[128,2048]{1,0:T(8,128)(2,1)S(1)} %get-tuple-element.48), channel_id=1, source_target_pairs={{0,18},{2,16},{4,22},{6,20},{8,26},{10,24},{12,30},{14,28},{16,2},... | collective-permute-start | bytes 1572872 | tf_op jit(solution)/shard_map/ppermute | solution.py:240
  156.9 61.2 %collective-permute-start.6 = (bf16[128,2048]{1,0:T(8,128)(2,1)}, bf16[128,2048]{1,0:T(8,128)(2,1)S(1)}, u32[]{:S(2)}, u32[]{:S(2)}) collective-permute-start(bf16[128,2048]{1,0:T(8,128)(2,1)} %get-tuple-element.47), channel_id=1, source_target_pairs={{0,4},{2,6},{4,0},{6,2},{8,12},{10,14},{12,8},{14,10},{16,20},{18,... | collective-permute-start | bytes 1572872 | tf_op jit(solution)/shard_map/ppermute | solution.py:240
  157.4 70.3 %collective-permute-start.8 = (bf16[128,2048]{1,0:T(8,128)(2,1)}, bf16[128,2048]{1,0:T(8,128)(2,1)S(1)}, u32[]{:S(2)}, u32[]{:S(2)}) collective-permute-start(bf16[128,2048]{1,0:T(8,128)(2,1)} %get-tuple-element.46), channel_id=1, source_target_pairs={{0,20},{2,22},{4,16},{6,18},{8,28},{10,30},{12,24},{14,26},{16,4},... | collective-permute-start | bytes 1572872 | tf_op jit(solution)/shard_map/ppermute | solution.py:240
  193.4 34.7 %collective-permute-start.9 = (bf16[128,2048]{1,0:T(8,128)(2,1)S(1)}, bf16[128,2048]{1,0:T(8,128)(2,1)S(1)}, u32[]{:S(2)}, u32[]{:S(2)}) collective-permute-start(bf16[128,2048]{1,0:T(8,128)(2,1)S(1)} %get-tuple-element.45), channel_id=1, source_target_pairs={{0,6},{2,4},{4,2},{6,0},{8,14},{10,12},{12,10},{14,8},{16,22},{18,... | collective-permute-start | bytes 1572872 | tf_op jit(solution)/shard_map/ppermute | solution.py:240
  194.5 55.1 %collective-permute-start.11 = (bf16[128,2048]{1,0:T(8,128)(2,1)S(1)}, bf16[128,2048]{1,0:T(8,128)(2,1)S(1)}, u32[]{:S(2)}, u32[]{:S(2)}) collective-permute-start(bf16[128,2048]{1,0:T(8,128)(2,1)S(1)} %get-tuple-element.44), channel_id=1, source_target_pairs={{0,22},{2,20},{4,18},{6,16},{8,30},{10,28},{12,26},{14,24},{16,6},... | collective-permute-start | bytes 1572872 | tf_op jit(solution)/shard_map/ppermute | solution.py:240
  215.8 57.8 %collective-permute-start.12 = (bf16[128,2048]{1,0:T(8,128)(2,1)S(1)}, bf16[128,2048]{1,0:T(8,128)(2,1)S(1)}, u32[]{:S(2)}, u32[]{:S(2)}) collective-permute-start(bf16[128,2048]{1,0:T(8,128)(2,1)S(1)} %get-tuple-element.43), channel_id=1, source_target_pairs={{0,8},{2,10},{4,12},{6,14},{8,0},{10,2},{12,4},{14,6},{16,24},{18,... | collective-permute-start | bytes 1572872 | tf_op jit(solution)/shard_map/ppermute | solution.py:240
  218.1 57.9 %collective-permute-start.14 = (bf16[128,2048]{1,0:T(8,128)(2,1)S(1)}, bf16[128,2048]{1,0:T(8,128)(2,1)S(1)}, u32[]{:S(2)}, u32[]{:S(2)}) collective-permute-start(bf16[128,2048]{1,0:T(8,128)(2,1)S(1)} %get-tuple-element.42), channel_id=1, source_target_pairs={{0,24},{2,26},{4,28},{6,30},{8,16},{10,18},{12,20},{14,22},{16,8},... | collective-permute-start | bytes 1572872 | tf_op jit(solution)/shard_map/ppermute | solution.py:240
  227.7 68.4 %collective-permute-start.15 = (bf16[128,2048]{1,0:T(8,128)(2,1)S(1)}, bf16[128,2048]{1,0:T(8,128)(2,1)S(1)}, u32[]{:S(2)}, u32[]{:S(2)}) collective-permute-start(bf16[128,2048]{1,0:T(8,128)(2,1)S(1)} %get-tuple-element.41), channel_id=1, source_target_pairs={{0,10},{2,8},{4,14},{6,12},{8,2},{10,0},{12,6},{14,4},{16,26},{18,... | collective-permute-start | bytes 1572872 | tf_op jit(solution)/shard_map/ppermute | solution.py:240
  228.1 69.6 %collective-permute-start.17 = (bf16[128,2048]{1,0:T(8,128)(2,1)S(1)}, bf16[128,2048]{1,0:T(8,128)(2,1)S(1)}, u32[]{:S(2)}, u32[]{:S(2)}) collective-permute-start(bf16[128,2048]{1,0:T(8,128)(2,1)S(1)} %get-tuple-element.40), channel_id=1, source_target_pairs={{0,26},{2,24},{4,30},{6,28},{8,18},{10,16},{12,22},{14,20},{16,10}... | collective-permute-start | bytes 1572872 | tf_op jit(solution)/shard_map/ppermute | solution.py:240
  249.6 71.5 %collective-permute-start.18 = (bf16[128,2048]{1,0:T(8,128)(2,1)S(1)}, bf16[128,2048]{1,0:T(8,128)(2,1)S(1)}, u32[]{:S(2)}, u32[]{:S(2)}) collective-permute-start(bf16[128,2048]{1,0:T(8,128)(2,1)S(1)} %get-tuple-element.39), channel_id=1, source_target_pairs={{0,12},{2,14},{4,8},{6,10},{8,4},{10,6},{12,0},{14,2},{16,28},{18,... | collective-permute-start | bytes 1572872 | tf_op jit(solution)/shard_map/ppermute | solution.py:240
  273.6 65.4 %collective-permute-start.20 = (bf16[128,2048]{1,0:T(8,128)(2,1)S(1)}, bf16[128,2048]{1,0:T(8,128)(2,1)S(1)}, u32[]{:S(2)}, u32[]{:S(2)}) collective-permute-start(bf16[128,2048]{1,0:T(8,128)(2,1)S(1)} %get-tuple-element.38), channel_id=1, source_target_pairs={{0,28},{2,30},{4,24},{6,26},{8,20},{10,22},{12,16},{14,18},{16,12}... | collective-permute-start | bytes 1572872 | tf_op jit(solution)/shard_map/ppermute | solution.py:240
  276.0 63.1 %collective-permute-start.21 = (bf16[128,2048]{1,0:T(8,128)(2,1)S(1)}, bf16[128,2048]{1,0:T(8,128)(2,1)S(1)}, u32[]{:S(2)}, u32[]{:S(2)}) collective-permute-start(bf16[128,2048]{1,0:T(8,128)(2,1)S(1)} %get-tuple-element.37), channel_id=1, source_target_pairs={{0,14},{2,12},{4,10},{6,8},{8,6},{10,4},{12,2},{14,0},{16,30},{18,... | collective-permute-start | bytes 1572872 | tf_op jit(solution)/shard_map/ppermute | solution.py:240
  296.1 45.7 %collective-permute-start.23 = (bf16[128,2048]{1,0:T(8,128)(2,1)S(1)}, bf16[128,2048]{1,0:T(8,128)(2,1)S(1)}, u32[]{:S(2)}, u32[]{:S(2)}) collective-permute-start(bf16[128,2048]{1,0:T(8,128)(2,1)S(1)} %fusion.14), channel_id=1, source_target_pairs={{0,30},{2,28},{4,26},{6,24},{8,22},{10,20},{12,18},{14,16},{16,14}... | collective-permute-start | bytes 1572872 | tf_op jit(solution)/shard_map/ppermute | solution.py:240
  (3 other events, 5.2 us)

commit v2 on v1

--- a/solution.py
+++ b/solution.py
@@ -24,12 +24,13 @@
 
 
 def mix_kernel(
-    slots, parts, width,
+    slots, parts, width, after_count,
     block_of, clean, lead_clean, core,
     q_ref, k_ref, v_ref, qp_ref, kp_ref, vp_ref, tails_ref, pos_ref, feat_ref, inner_ref, w_hbm,
     *rest,
 ):
-    outs, (qx, kx, vx, gx, mixed, w_ref, sem) = rest[:-7], rest[-7:]
+    scratch, outs = rest[-7:], rest[after_count:-7]
+    qx, kx, vx, gx, mixed, w_ref, sem = scratch
     slot = pl.program_id(0)
     block_rows, channels = q_ref.shape
     tiles = block_rows // TILE
@@ -48,74 +49,73 @@
 
     @pl.when(block >= 0)
     def _():
-        def one_chunk(c, carry):
+        at_start = block == 0
+
+        def one_chunk(masked, c, carry):
             lanes = pl.ds(pl.multiple_of(c * LANES, LANES), LANES)
             for i, (dst, src, before) in enumerate(
                 ((qx, q_ref, qp_ref), (kx, k_ref, kp_ref), (vx, v_ref, vp_ref))
             ):
+                tail = tails_ref[i, :, lanes].astype(jnp.float32)
+                dst[:LEAD, :] = jnp.where(at_start, tail, before[:, lanes].astype(jnp.float32))
                 dst[LEAD:, :] = src[:, lanes].astype(jnp.float32)
-
-                @pl.when(block == 0)
-                def _():
-                    dst[:LEAD, :] = tails_ref[i, :, lanes].astype(jnp.float32)
-
-                @pl.when(block > 0)
-                def _():
-                    dst[:LEAD, :] = before[:, lanes].astype(jnp.float32)
 
             feat = [[feat_ref[i, t : t + 1, lanes] for t in range(TAPS)] for i in range(3)]
             inner = [inner_ref[t : t + 1, lanes] for t in range(TAPS)]
-
-            def lead(masked):
-                rows = 8
-                positions = None
-                if masked:
-                    positions = pos_ref[0:1, :] - (
-                        rows - lax.broadcasted_iota(jnp.int32, (rows, LANES), 0)
-                    )
-                gx[0:rows, :] = taps_sum(kx, LEAD - rows, rows, feat[1], positions) * taps_sum(
-                    vx, LEAD - rows, rows, feat[2], positions
+            rows = 8
+            positions = None
+            if masked:
+                positions = pos_ref[0:1, :] - (
+                    rows - lax.broadcasted_iota(jnp.int32, (rows, LANES), 0)
                 )
-
-            @pl.when(lead_clean[block] > 0)
-            def _():
-                lead(False)
-
-            @pl.when(lead_clean[block] == 0)
-            def _():
-                lead(True)
-
-            def tile_of(t, masked):
-                first = t * TILE
-                positions = pos_ref[first : first + TILE, :] if masked else None
-                gx[8 + first : 8 + first + TILE, :] = taps_sum(
-                    kx, LEAD + first, TILE, feat[1], positions
-                ) * taps_sum(vx, LEAD + first, TILE, feat[2], positions)
-                query = taps_sum(qx, LEAD + first, TILE, feat[0], positions)
-                result = query * taps_sum(gx, 8 + first, TILE, inner, positions)
-                mixed[pl.ds(pl.multiple_of(base + first, TILE), TILE), lanes] = result.astype(
+            gx[0:rows, :] = taps_sum(kx, LEAD - rows, rows, feat[1], positions) * taps_sum(
+                vx, LEAD - rows, rows, feat[2], positions
+            )
+
+            def tile_of(first, rows, masked):
+                positions = pos_ref[first : first + rows, :] if masked else None
+                gx[8 + first : 8 + first + rows, :] = taps_sum(
+                    kx, LEAD + first, rows, feat[1], positions
+                ) * taps_sum(vx, LEAD + first, rows, feat[2], positions)
+                query = taps_sum(qx, LEAD + first, rows, feat[0], positions)
+                result = query * taps_sum(gx, 8 + first, rows, inner, positions)
+                mixed[pl.ds(pl.multiple_of(base + first, TILE), rows), lanes] = result.astype(
                     mixed.dtype
                 )
 
+            if not masked:
+                for t in range(tiles):
+                    tile_of(t * TILE, TILE, False)
+                return carry
             for t in range(tiles):
                 flag = clean[block * tiles + t]
 
                 @pl.when(flag > 0)
                 def _():
-                    tile_of(t, False)
+                    tile_of(t * TILE, TILE, False)
 
                 @pl.when(flag == 0)
                 def _():
-                    tile_of(t, True)
+                    tile_of(t * TILE, TILE, True)
 
             return carry
 
-        lax.fori_loop(0, channels // LANES, one_chunk, 0)
+        whole_clean = lead_clean[block]
+        for t in range(tiles):
+            whole_clean = whole_clean * clean[block * tiles + t]
+
+        @pl.when(whole_clean > 0)
+        def _():
+            lax.fori_loop(0, channels // LANES, functools.partial(one_chunk, False), 0)
+
+        @pl.when(whole_clean == 0)
+        def _():
+            lax.fori_loop(0, channels // LANES, functools.partial(one_chunk, True), 0)
 
     @pl.when(slot == slots - 1)
     def _():
         w_copy.wait()
-        step = min(width, 512)
+        step = min(width, 1024)
         for j in range(parts):
             first = lax.rem(core[0] + j, parts) * width if len(outs) > 1 else j * width
 
@@ -135,7 +135,7 @@
             lax.fori_loop(0, width // step, columns, 0)
 
 
-def mix_blocks(scalars, streams, tails, positions, feat_filter, inner_filter, out_weight, parts, block_rows):
+def mix_blocks(scalars, streams, tails, positions, feat_filter, inner_filter, out_weight, parts, block_rows, after):
     slots = scalars[0].shape[0]
     rows, channels = streams[0].shape
     width = out_weight.shape[1] // parts
@@ -155,7 +155,7 @@
         shapes = [jax.ShapeDtypeStruct((parts, slots * block_rows, width), jnp.bfloat16)]
     filled_flops = 2 * slots * block_rows * channels * out_weight.shape[1]
     return pl.pallas_call(
-        functools.partial(mix_kernel, slots, parts, width),
+        functools.partial(mix_kernel, slots, parts, width, len(after)),
         out_shape=shapes,
         grid_spec=pltpu.PrefetchScalarGridSpec(
             num_scalar_prefetch=4,
@@ -167,8 +167,8 @@
                 pl.BlockSpec((block_rows, LANES), here),
                 whole(feat_filter.shape),
                 whole(inner_filter.shape),
-                pl.BlockSpec(memory_space=pl.ANY),
-            ],
+            ]
+            + [pl.BlockSpec(memory_space=pl.ANY)] * (1 + len(after)),
             out_specs=[whole(s.shape) for s in shapes],
             scratch_shapes=[pltpu.VMEM((LEAD + block_rows, LANES), jnp.float32)] * 3
             + [
@@ -184,7 +184,20 @@
         cost_estimate=pl.CostEstimate(
             flops=filled_flops, bytes_accessed=16 * 1024 * 1024 + slots * 6 * 1024 * 1024, transcendentals=0
         ),
-    )(*scalars, *streams, *streams, tails, positions, feat_filter, inner_filter, out_weight)
+    )(*scalars, *streams, *streams, tails, positions, feat_filter, inner_filter, out_weight, *after)
+
+
+def unset_kernel(out):
+    pass
+
+
+def unset(shape, dtype):
+    return pl.pallas_call(
+        unset_kernel,
+        out_shape=jax.ShapeDtypeStruct(shape, dtype),
+        out_specs=pl.BlockSpec(memory_space=pl.ANY),
+        cost_estimate=pl.CostEstimate(flops=0, bytes_accessed=0, transcendentals=0),
+    )()
 
 
 def per_device(
@@ -210,19 +223,26 @@
     lead_clean = (doc_pos.reshape(block_count, block_rows)[:, 0] >= 2 * (TAPS - 1)).astype(jnp.int32)
 
     half = dp_count // 2
-    order = [r for pair in zip(range(half, dp_count), list(range(1, half)) + [0]) for r in pair]
+    far, near = list(range(half, dp_count)), list(range(1, half)) + [0]
+    order = far[:1] + [r for pair in zip(far[1:], near) for r in pair] + near[half - 1 :]
+    sizes = [1] + [2] * (half - 2) + [3]
     partner = jnp.bitwise_xor(me.astype(jnp.int32), jnp.asarray(order, jnp.int32))
     numbers = jnp.arange(block_count, dtype=jnp.int32)
     named = (destination[:, 0][None, :] == partner[:, None]) & (numbers < counts[0])[None, :]
     block_of = jnp.max(jnp.where(named, numbers[None, :], -1), axis=1)
 
-    result = jnp.zeros((dp_count, block_rows, width), jnp.bfloat16)
-    group = 2
-    for first in range(0, dp_count, group):
+    ready = []
+    arrived = []
+    result = unset((dp_count, block_rows, width), jnp.bfloat16)
+    first = 0
+    for group in sizes:
         terms = mix_blocks(
             (block_of[first : first + group], clean, lead_clean, core),
             streams, tails, positions, feat_filter, inner_filter, out_weight, tp_count, block_rows,
+            ready[-2] if len(ready) > 1 else [],
         )
+        ready.append([])
+        arrived.append([])
         if tp_count == 2:
             other = lax.ppermute(terms[1], "tensor", [(0, 1), (1, 0)])
         else:
@@ -236,9 +256,12 @@
                 ).astype(jnp.bfloat16)
             else:
                 block = summed[s]
+            ready[-1].append(block)
             if r:
                 block = lax.ppermute(block, "dp", [(i, i ^ r) for i in range(dp_count)])
+                arrived[-1].append(block)
             result = lax.dynamic_update_index_in_dim(result, block, jnp.bitwise_xor(me, r), 0)
+        first += group
     return result.reshape(dp_count * block_rows, width)
 
 

time: 349 us -> 260 us (0.74)
  waiting for transfers between devices: 150 us -> 84.2 us
  Pallas kernels: 124 us -> 109 us
  starting transfers between devices: 47.3 us -> 35.7 us
  local copies, waits for them, and re-layouts: 10.5 us -> 17.9 us
  other arithmetic: 12.9 us -> 8.47 us
    ppermute x15, waiting for transfers between devices: 147 us -> 81.2 us  [per_device(): block = lax.ppermute(block, 'dp', [(i, i ^ r) for i in range(dp_count)])]
    pallas_call x8 -> x9, Pallas kernels: 124 us -> 109 us  [the longest x8 109 us: mix_blocks(): pl.pallas_call(functools.partial(mix_kernel, slots, parts, width, len(aft...]
    dynamic_update_slice x15, local copies, waits for them, and re-layouts: 0.79 us -> 12.6 us  [per_device(): lax.dynamic_update_index_in_dim(result, block, jnp.bitwise_xor(me, r), 0)]
    ppermute x15, starting transfers between devices: 41.5 us -> 31.3 us  [per_device(): block = lax.ppermute(block, 'dp', [(i, i ^ r) for i in range(dp_count)])]
    convert_element_type x8, other arithmetic: 10.3 us -> 5.08 us  [per_device(): block = (terms[0][s].astype(jnp.float32) + other[s].astype(jnp.float32))....]
  transfers between devices with their start and end apart: 24 -> 24, of which waited for: 12 -> 9; matrix products, arithmetic and copies ran while one was open for 4% -> 8% of each run, Pallas kernels for 31% -> 38%
where the time goes in v2:
time: 260 us; the launch traced here: 257 us
  Pallas kernels  109 us (42%)
  waiting for transfers between devices  84.2 us (32%)
  starting transfers between devices  35.7 us (14%)
  local copies, waits for them, and re-layouts  17.9 us (7%)
  other arithmetic  8.47 us (3%)
    pallas_call x8, Pallas kernels, mix_blocks(): pl.pallas_call(functools.partial(mix_kernel, slots, parts, width, len(aft...  109 us
    ppermute x15, waiting for transfers between devices, per_device(): block = lax.ppermute(block, 'dp', [(i, i ^ r) for i in range(dp_count)])  81.2 us
    ppermute x15, starting transfers between devices, per_device(): block = lax.ppermute(block, 'dp', [(i, i ^ r) for i in range(dp_count)])  31.3 us
    dynamic_update_slice x15, local copies, waits for them, and re-layouts, per_device(): lax.dynamic_update_index_in_dim(result, block, jnp.bitwise_xor(me, r), 0)  12.6 us
  transfers between devices with their start and end apart: 24, of which 9 were waited for; matrix products, arithmetic and copies ran while one was open for 8% of the time, Pallas kernels for 38%

profile of v2, /device:TPU:16, one launch (start us, length us, event | category | flops | bytes accessed | tf_op | source)
XLA Modules:
  0.0 256.7 jit_solution(13146357784584398078)
XLA Ops:
  1.8 3.4 %collective-permute-start = (bf16[3,16,2048]{2,1,0:T(8,128)(2,1)S(1)}, bf16[3,16,2048]{2,1,0:T(8,128)(2,1)S(1)}, u32[]{:S(2)}, u32[]{:S(2)}) collective-permute-start(bf16[3,16,2048]{2,1,0:T(8,128)(2,1)S(1)} %pad_maximum_fusion), channel_id=1, source_target_pairs={{0,2},{2,4},{4,6},{6,8},{8,10},{10,12},{12,14},{14,16},{16,18},{18... | collective-permute-start | bytes 589832 | tf_op jit(solution)/shard_map/ppermute | solution.py:216
  9.1 3.0 %collective-permute-done.tails_ref = bf16[3,16,2048]{2,1,0:T(8,128)(2,1)S(1)} collective-permute-done((bf16[3,16,2048]{2,1,0:T(8,128)(2,1)S(1)}, bf16[3,16,2048]{2,1,0:T(8,128)(2,1)S(1)}, u32[]{:S(2)}, u32[]{:S(2)}) %collective-permute-start) | collective-permute-done | bytes 196640 | tf_op jit(solution)/shard_map/ppermute | solution.py:216
  14.8 10.7 %shard_map.101 = (bf16[1,128,2048]{2,1,0:T(8,128)(2,1)S(1)}, bf16[1,128,2048]{2,1,0:T(8,128)(2,1)S(1)}) custom-call(s32[1]{0:T(128)S(1)} %bitcast.73, s32[48]{0:T(128)S(1)} %compare_convert_fusion.clean, s32[12]{0:T(128)S(1)} %convert_reduce_fusion.lead_clean, s32[1]{0:T(128)} %bitcast.3.core, bf16[1536,2048]{1,0:T(8,128)(2,1)} %qp_ref.15, ...), custom_call_target="tpu_custom_call" | custom-call | flops 2147483648 | bytes 23068672 | tf_op jit(solution)/shard_map/pallas_call | solution.py:157
  25.7 13.9 %shard_map.102 = (bf16[2,128,2048]{2,1,0:T(8,128)(2,1)S(1)}, bf16[2,128,2048]{2,1,0:T(8,128)(2,1)}) custom-call(s32[2]{0:T(128)S(1)} %get-tuple-element.56.block_of, s32[48]{0:T(128)S(1)} %compare_convert_fusion.clean, s32[12]{0:T(128)S(1)} %convert_reduce_fusion.lead_clean, s32[1]{0:T(128)} %bitcast.3.core, bf16[1536,2048]{1,0:T(8,128)(2,1)} %qp_ref.15, ...), custom_call_target="tpu_custom_call" | custom-call | flops 4294967296 | bytes 29360128 | tf_op jit(solution)/shard_map/pallas_call | solution.py:157
  41.5 13.8 %shard_map.103 = (bf16[2,128,2048]{2,1,0:T(8,128)(2,1)S(1)}, bf16[2,128,2048]{2,1,0:T(8,128)(2,1)S(1)}) custom-call(s32[2]{0:T(128)S(1)} %get-tuple-element.55.block_of, s32[48]{0:T(128)S(1)} %compare_convert_fusion.clean, s32[12]{0:T(128)S(1)} %convert_reduce_fusion.lead_clean, s32[1]{0:T(128)} %bitcast.3.core, bf16[1536,2048]{1,0:T(8,128)(2,1)} %qp_ref.15, ...), custom_call_target="tpu_custom_call" | custom-call | flops 4294967296 | bytes 29360128 | tf_op jit(solution)/shard_map/pallas_call | solution.py:157
  57.1 2.0 collective-permute-start.4
  61.1 13.8 %shard_map.104 = (bf16[2,128,2048]{2,1,0:T(8,128)(2,1)S(1)}, bf16[2,128,2048]{2,1,0:T(8,128)(2,1)S(1)}) custom-call(s32[2]{0:T(128)S(1)} %get-tuple-element.54.block_of, s32[48]{0:T(128)S(1)} %compare_convert_fusion.clean, s32[12]{0:T(128)S(1)} %convert_reduce_fusion.lead_clean, s32[1]{0:T(128)} %bitcast.3.core, bf16[1536,2048]{1,0:T(8,128)(2,1)} %qp_ref.15, ...), custom_call_target="tpu_custom_call" | custom-call | flops 4294967296 | bytes 29360128 | tf_op jit(solution)/shard_map/pallas_call | solution.py:157
  77.4 4.0 %collective-permute-start.7 = (bf16[128,2048]{1,0:T(8,128)(2,1)S(1)}, bf16[128,2048]{1,0:T(8,128)(2,1)S(1)}, u32[]{:S(2)}, u32[]{:S(2)}) collective-permute-start(bf16[128,2048]{1,0:T(8,128)(2,1)S(1)} %get-tuple-element.48.rest_0_), channel_id=1, source_target_pairs={{0,20},{2,22},{4,16},{6,18},{8,28},{10,30},{12,24},{14,26},{16,4},... | collective-permute-start | bytes 1572872 | tf_op jit(solution)/shard_map/ppermute | solution.py:261
  82.4 13.6 %shard_map.105 = (bf16[2,128,2048]{2,1,0:T(8,128)(2,1)S(1)}, bf16[2,128,2048]{2,1,0:T(8,128)(2,1)S(1)}) custom-call(s32[2]{0:T(128)S(1)} %get-tuple-element.53.block_of, s32[48]{0:T(128)S(1)} %compare_convert_fusion.clean, s32[12]{0:T(128)S(1)} %convert_reduce_fusion.lead_clean, s32[1]{0:T(128)} %bitcast.3.core, bf16[1536,2048]{1,0:T(8,128)(2,1)} %qp_ref.15, ...), custom_call_target="tpu_custom_call" | custom-call | flops 4294967296 | bytes 29360128 | tf_op jit(solution)/shard_map/pallas_call | solution.py:157
  95.9 2.8 %collective-permute-done.4 = bf16[128,2048]{1,0:T(8,128)(2,1)S(1)} collective-permute-done((bf16[128,2048]{1,0:T(8,128)(2,1)S(1)}, bf16[128,2048]{1,0:T(8,128)(2,1)S(1)}, u32[]{:S(2)}, u32[]{:S(2)}) %collective-permute-start.4) | collective-permute-done | bytes 524320 | tf_op jit(solution)/shard_map/ppermute | solution.py:261
  100.8 4.9 %collective-permute-start.10 = (bf16[128,2048]{1,0:T(8,128)(2,1)S(1)}, bf16[128,2048]{1,0:T(8,128)(2,1)S(1)}, u32[]{:S(2)}, u32[]{:S(2)}) collective-permute-start(bf16[128,2048]{1,0:T(8,128)(2,1)S(1)} %get-tuple-element.46.rest_0_), channel_id=1, source_target_pairs={{0,22},{2,20},{4,18},{6,16},{8,30},{10,28},{12,26},{14,24},{16,6},... | collective-permute-start | bytes 1572872 | tf_op jit(solution)/shard_map/ppermute | solution.py:261
  106.1 13.5 %shard_map.106 = (bf16[2,128,2048]{2,1,0:T(8,128)(2,1)S(1)}, bf16[2,128,2048]{2,1,0:T(8,128)(2,1)S(1)}) custom-call(s32[2]{0:T(128)S(1)} %get-tuple-element.52.block_of, s32[48]{0:T(128)S(1)} %compare_convert_fusion.clean, s32[12]{0:T(128)S(1)} %convert_reduce_fusion.lead_clean, s32[1]{0:T(128)} %bitcast.3.core, bf16[1536,2048]{1,0:T(8,128)(2,1)} %qp_ref.15, ...), custom_call_target="tpu_custom_call" | custom-call | flops 4294967296 | bytes 29360128 | tf_op jit(solution)/shard_map/pallas_call | solution.py:157
  119.6 2.2 collective-permute-done.7
  123.4 9.0 %collective-permute-done.10 = bf16[128,2048]{1,0:T(8,128)(2,1)S(1)} collective-permute-done((bf16[128,2048]{1,0:T(8,128)(2,1)S(1)}, bf16[128,2048]{1,0:T(8,128)(2,1)S(1)}, u32[]{:S(2)}, u32[]{:S(2)}) %collective-permute-start.10) | collective-permute-done | bytes 524320 | tf_op jit(solution)/shard_map/ppermute | solution.py:261
  134.5 2.6 %collective-permute-start.13 = (bf16[128,2048]{1,0:T(8,128)(2,1)S(1)}, bf16[128,2048]{1,0:T(8,128)(2,1)S(1)}, u32[]{:S(2)}, u32[]{:S(2)}) collective-permute-start(bf16[128,2048]{1,0:T(8,128)(2,1)S(1)} %get-tuple-element.44.rest_0_), channel_id=1, source_target_pairs={{0,24},{2,26},{4,28},{6,30},{8,16},{10,18},{12,20},{14,22},{16,8},... | collective-permute-start | bytes 1572872 | tf_op jit(solution)/shard_map/ppermute | solution.py:261
  137.2 2.8 %collective-permute-start.14 = (bf16[128,2048]{1,0:T(8,128)(2,1)S(1)}, bf16[128,2048]{1,0:T(8,128)(2,1)S(1)}, u32[]{:S(2)}, u32[]{:S(2)}) collective-permute-start(bf16[128,2048]{1,0:T(8,128)(2,1)S(1)} %get-tuple-element.43.rest_1_), channel_id=1, source_target_pairs={{0,8},{2,10},{4,12},{6,14},{8,0},{10,2},{12,4},{14,6},{16,24},{18,... | collective-permute-start | bytes 1572872 | tf_op jit(solution)/shard_map/ppermute | solution.py:261
  140.0 13.1 %shard_map.107 = (bf16[2,128,2048]{2,1,0:T(8,128)(2,1)S(1)}, bf16[2,128,2048]{2,1,0:T(8,128)(2,1)S(1)}) custom-call(s32[2]{0:T(128)S(1)} %get-tuple-element.51.block_of, s32[48]{0:T(128)S(1)} %compare_convert_fusion.clean, s32[12]{0:T(128)S(1)} %convert_reduce_fusion.lead_clean, s32[1]{0:T(128)} %bitcast.3.core, bf16[1536,2048]{1,0:T(8,128)(2,1)} %qp_ref.15, ...), custom_call_target="tpu_custom_call" | custom-call | flops 4294967296 | bytes 29360128 | tf_op jit(solution)/shard_map/pallas_call | solution.py:157
  153.6 4.3 %collective-permute-start.16 = (bf16[128,2048]{1,0:T(8,128)(2,1)S(1)}, bf16[128,2048]{1,0:T(8,128)(2,1)S(1)}, u32[]{:S(2)}, u32[]{:S(2)}) collective-permute-start(bf16[128,2048]{1,0:T(8,128)(2,1)S(1)} %get-tuple-element.42.rest_0_), channel_id=1, source_target_pairs={{0,26},{2,24},{4,30},{6,28},{8,18},{10,16},{12,22},{14,20},{16,10}... | collective-permute-start | bytes 1572872 | tf_op jit(solution)/shard_map/ppermute | solution.py:261
  158.3 17.1 %shard_map.108 = (bf16[3,128,2048]{2,1,0:T(8,128)(2,1)S(1)}, bf16[3,128,2048]{2,1,0:T(8,128)(2,1)S(1)}) custom-call(s32[3]{0:T(128)S(1)} %slice.161.block_of, s32[48]{0:T(128)S(1)} %compare_convert_fusion.clean, s32[12]{0:T(128)S(1)} %convert_reduce_fusion.lead_clean, s32[1]{0:T(128)} %bitcast.3.core, bf16[1536,2048]{1,0:T(8,128)(2,1)} %qp_ref.15, ...), custom_call_target="tpu_custom_call" | custom-call | flops 6442450944 | bytes 35651584 | tf_op jit(solution)/shard_map/pallas_call | solution.py:157
  177.2 11.9 %collective-permute-done.16 = bf16[128,2048]{1,0:T(8,128)(2,1)S(1)} collective-permute-done((bf16[128,2048]{1,0:T(8,128)(2,1)S(1)}, bf16[128,2048]{1,0:T(8,128)(2,1)S(1)}, u32[]{:S(2)}, u32[]{:S(2)}) %collective-permute-start.16) | collective-permute-done | bytes 524320 | tf_op jit(solution)/shard_map/ppermute | solution.py:261
  190.3 3.6 %collective-permute-start.19 = (bf16[128,2048]{1,0:T(8,128)(2,1)S(1)}, bf16[128,2048]{1,0:T(8,128)(2,1)S(1)}, u32[]{:S(2)}, u32[]{:S(2)}) collective-permute-start(bf16[128,2048]{1,0:T(8,128)(2,1)S(1)} %get-tuple-element.40), channel_id=1, source_target_pairs={{0,28},{2,30},{4,24},{6,26},{8,20},{10,22},{12,16},{14,18},{16,12}... | collective-permute-start | bytes 1572872 | tf_op jit(solution)/shard_map/ppermute | solution.py:261
  195.2 3.2 %collective-permute-start.22 = (bf16[128,2048]{1,0:T(8,128)(2,1)S(1)}, bf16[128,2048]{1,0:T(8,128)(2,1)S(1)}, u32[]{:S(2)}, u32[]{:S(2)}) collective-permute-start(bf16[128,2048]{1,0:T(8,128)(2,1)S(1)} %get-tuple-element.38), channel_id=1, source_target_pairs={{0,30},{2,28},{4,26},{6,24},{8,22},{10,20},{12,18},{14,16},{16,14}... | collective-permute-start | bytes 1572872 | tf_op jit(solution)/shard_map/ppermute | solution.py:261
  198.4 33.7 %collective-permute-done.19 = bf16[128,2048]{1,0:T(8,128)(2,1)S(1)} collective-permute-done((bf16[128,2048]{1,0:T(8,128)(2,1)S(1)}, bf16[128,2048]{1,0:T(8,128)(2,1)S(1)}, u32[]{:S(2)}, u32[]{:S(2)}) %collective-permute-start.19) | collective-permute-done | bytes 524320 | tf_op jit(solution)/shard_map/ppermute | solution.py:261
  233.7 18.5 %collective-permute-done.22 = bf16[128,2048]{1,0:T(8,128)(2,1)S(1)} collective-permute-done((bf16[128,2048]{1,0:T(8,128)(2,1)S(1)}, bf16[128,2048]{1,0:T(8,128)(2,1)S(1)}, u32[]{:S(2)}, u32[]{:S(2)}) %collective-permute-start.22) | collective-permute-done | bytes 524320 | tf_op jit(solution)/shard_map/ppermute | solution.py:261
  (78 shorter events, 34.5 us)
Async XLA Ops:
  1.8 10.3 %collective-permute-start = (bf16[3,16,2048]{2,1,0:T(8,128)(2,1)S(1)}, bf16[3,16,2048]{2,1,0:T(8,128)(2,1)S(1)}, u32[]{:S(2)}, u32[]{:S(2)}) collective-permute-start(bf16[3,16,2048]{2,1,0:T(8,128)(2,1)S(1)} %pad_maximum_fusion), channel_id=1, source_target_pairs={{0,2},{2,4},{4,6},{6,8},{8,10},{10,12},{12,14},{14,16},{16,18},{18... | collective-permute-start | bytes 589832 | tf_op jit(solution)/shard_map/ppermute | solution.py:216
  25.6 14.7 %collective-permute-start.1 = (bf16[1,128,2048]{2,1,0:T(8,128)(2,1)S(1)}, bf16[1,128,2048]{2,1,0:T(8,128)(2,1)}, u32[]{:S(2)}, u32[]{:S(2)}) collective-permute-start(bf16[1,128,2048]{2,1,0:T(8,128)(2,1)S(1)} %get-tuple-element.22), channel_id=1, source_target_pairs={{0,1},{1,0},{2,3},{3,2},{4,5},{5,4},{6,7},{7,6},{8,9},{9,8},{10,11... | collective-permute-start | bytes 1572872 | tf_op jit(solution)/shard_map/ppermute | solution.py:247
  39.6 15.9 %collective-permute-start.3 = (bf16[2,128,2048]{2,1,0:T(8,128)(2,1)}, bf16[2,128,2048]{2,1,0:T(8,128)(2,1)}, u32[]{:S(2)}, u32[]{:S(2)}) collective-permute-start(bf16[2,128,2048]{2,1,0:T(8,128)(2,1)} %get-tuple-element.24), channel_id=1, source_target_pairs={{0,1},{1,0},{2,3},{3,2},{4,5},{5,4},{6,7},{7,6},{8,9},{9,8},{10,11... | collective-permute-start | bytes 3145736 | tf_op jit(solution)/shard_map/ppermute | solution.py:247
  41.4 34.8 %collective-permute-start.2 = (bf16[128,2048]{1,0:T(8,128)(2,1)S(1)}, bf16[128,2048]{1,0:T(8,128)(2,1)S(1)}, u32[]{:S(2)}, u32[]{:S(2)}) collective-permute-start(bf16[128,2048]{1,0:T(8,128)(2,1)S(1)} %fusion.rest_0_), channel_id=1, source_target_pairs={{0,16},{2,18},{4,20},{6,22},{8,24},{10,26},{12,28},{14,30},{16,0},... | collective-permute-start | bytes 1572872 | tf_op jit(solution)/shard_map/ppermute | solution.py:261
  55.3 21.7 %collective-permute-start.6 = (bf16[2,128,2048]{2,1,0:T(8,128)(2,1)S(1)}, bf16[2,128,2048]{2,1,0:T(8,128)(2,1)S(1)}, u32[]{:S(2)}, u32[]{:S(2)}) collective-permute-start(bf16[2,128,2048]{2,1,0:T(8,128)(2,1)S(1)} %get-tuple-element.26), channel_id=1, source_target_pairs={{0,1},{1,0},{2,3},{3,2},{4,5},{5,4},{6,7},{7,6},{8,9},{9,8},{10,11... | collective-permute-start | bytes 3145736 | tf_op jit(solution)/shard_map/ppermute | solution.py:247
  57.1 41.6 %collective-permute-start.4 = (bf16[128,2048]{1,0:T(8,128)(2,1)S(1)}, bf16[128,2048]{1,0:T(8,128)(2,1)S(1)}, u32[]{:S(2)}, u32[]{:S(2)}) collective-permute-start(bf16[128,2048]{1,0:T(8,128)(2,1)S(1)} %get-tuple-element.50.rest_0_), channel_id=1, source_target_pairs={{0,18},{2,16},{4,22},{6,20},{8,26},{10,24},{12,30},{14,28},{16,2},... | collective-permute-start | bytes 1572872 | tf_op jit(solution)/shard_map/ppermute | solution.py:261
  59.1 40.4 %collective-permute-start.5 = (bf16[128,2048]{1,0:T(8,128)(2,1)S(1)}, bf16[128,2048]{1,0:T(8,128)(2,1)S(1)}, u32[]{:S(2)}, u32[]{:S(2)}) collective-permute-start(bf16[128,2048]{1,0:T(8,128)(2,1)S(1)} %get-tuple-element.49.rest_1_), channel_id=1, source_target_pairs={{0,2},{2,0},{4,6},{6,4},{8,10},{10,8},{12,14},{14,12},{16,18},{18,... | collective-permute-start | bytes 1572872 | tf_op jit(solution)/shard_map/ppermute | solution.py:261
  74.9 25.4 %collective-permute-start.9 = (bf16[2,128,2048]{2,1,0:T(8,128)(2,1)S(1)}, bf16[2,128,2048]{2,1,0:T(8,128)(2,1)S(1)}, u32[]{:S(2)}, u32[]{:S(2)}) collective-permute-start(bf16[2,128,2048]{2,1,0:T(8,128)(2,1)S(1)} %get-tuple-element.28), channel_id=1, source_target_pairs={{0,1},{1,0},{2,3},{3,2},{4,5},{5,4},{6,7},{7,6},{8,9},{9,8},{10,11... | collective-permute-start | bytes 3145736 | tf_op jit(solution)/shard_map/ppermute | solution.py:247
  77.4 44.3 %collective-permute-start.7 = (bf16[128,2048]{1,0:T(8,128)(2,1)S(1)}, bf16[128,2048]{1,0:T(8,128)(2,1)S(1)}, u32[]{:S(2)}, u32[]{:S(2)}) collective-permute-start(bf16[128,2048]{1,0:T(8,128)(2,1)S(1)} %get-tuple-element.48.rest_0_), channel_id=1, source_target_pairs={{0,20},{2,22},{4,16},{6,18},{8,28},{10,30},{12,24},{14,26},{16,4},... | collective-permute-start | bytes 1572872 | tf_op jit(solution)/shard_map/ppermute | solution.py:261
  81.4 41.2 %collective-permute-start.8 = (bf16[128,2048]{1,0:T(8,128)(2,1)S(1)}, bf16[128,2048]{1,0:T(8,128)(2,1)S(1)}, u32[]{:S(2)}, u32[]{:S(2)}) collective-permute-start(bf16[128,2048]{1,0:T(8,128)(2,1)S(1)} %get-tuple-element.47.rest_1_), channel_id=1, source_target_pairs={{0,4},{2,6},{4,0},{6,2},{8,12},{10,14},{12,8},{14,10},{16,20},{18,... | collective-permute-start | bytes 1572872 | tf_op jit(solution)/shard_map/ppermute | solution.py:261
  98.7 35.5 %collective-permute-start.12 = (bf16[2,128,2048]{2,1,0:T(8,128)(2,1)S(1)}, bf16[2,128,2048]{2,1,0:T(8,128)(2,1)S(1)}, u32[]{:S(2)}, u32[]{:S(2)}) collective-permute-start(bf16[2,128,2048]{2,1,0:T(8,128)(2,1)S(1)} %get-tuple-element.30), channel_id=1, source_target_pairs={{0,1},{1,0},{2,3},{3,2},{4,5},{5,4},{6,7},{7,6},{8,9},{9,8},{10,11... | collective-permute-start | bytes 3145736 | tf_op jit(solution)/shard_map/ppermute | solution.py:247
  100.8 31.7 %collective-permute-start.10 = (bf16[128,2048]{1,0:T(8,128)(2,1)S(1)}, bf16[128,2048]{1,0:T(8,128)(2,1)S(1)}, u32[]{:S(2)}, u32[]{:S(2)}) collective-permute-start(bf16[128,2048]{1,0:T(8,128)(2,1)S(1)} %get-tuple-element.46.rest_0_), channel_id=1, source_target_pairs={{0,22},{2,20},{4,18},{6,16},{8,30},{10,28},{12,26},{14,24},{16,6},... | collective-permute-start | bytes 1572872 | tf_op jit(solution)/shard_map/ppermute | solution.py:261
  105.6 27.7 %collective-permute-start.11 = (bf16[128,2048]{1,0:T(8,128)(2,1)S(1)}, bf16[128,2048]{1,0:T(8,128)(2,1)S(1)}, u32[]{:S(2)}, u32[]{:S(2)}) collective-permute-start(bf16[128,2048]{1,0:T(8,128)(2,1)S(1)} %get-tuple-element.45.rest_1_), channel_id=1, source_target_pairs={{0,6},{2,4},{4,2},{6,0},{8,14},{10,12},{12,10},{14,8},{16,22},{18,... | collective-permute-start | bytes 1572872 | tf_op jit(solution)/shard_map/ppermute | solution.py:261
  121.8 31.4 %collective-permute-start.15 = (bf16[2,128,2048]{2,1,0:T(8,128)(2,1)S(1)}, bf16[2,128,2048]{2,1,0:T(8,128)(2,1)S(1)}, u32[]{:S(2)}, u32[]{:S(2)}) collective-permute-start(bf16[2,128,2048]{2,1,0:T(8,128)(2,1)S(1)} %get-tuple-element.32), channel_id=1, source_target_pairs={{0,1},{1,0},{2,3},{3,2},{4,5},{5,4},{6,7},{7,6},{8,9},{9,8},{10,11... | collective-permute-start | bytes 3145736 | tf_op jit(solution)/shard_map/ppermute | solution.py:247
  134.5 40.8 %collective-permute-start.13 = (bf16[128,2048]{1,0:T(8,128)(2,1)S(1)}, bf16[128,2048]{1,0:T(8,128)(2,1)S(1)}, u32[]{:S(2)}, u32[]{:S(2)}) collective-permute-start(bf16[128,2048]{1,0:T(8,128)(2,1)S(1)} %get-tuple-element.44.rest_0_), channel_id=1, source_target_pairs={{0,24},{2,26},{4,28},{6,30},{8,16},{10,18},{12,20},{14,22},{16,8},... | collective-permute-start | bytes 1572872 | tf_op jit(solution)/shard_map/ppermute | solution.py:261
  137.2 39.1 %collective-permute-start.14 = (bf16[128,2048]{1,0:T(8,128)(2,1)S(1)}, bf16[128,2048]{1,0:T(8,128)(2,1)S(1)}, u32[]{:S(2)}, u32[]{:S(2)}) collective-permute-start(bf16[128,2048]{1,0:T(8,128)(2,1)S(1)} %get-tuple-element.43.rest_1_), channel_id=1, source_target_pairs={{0,8},{2,10},{4,12},{6,14},{8,0},{10,2},{12,4},{14,6},{16,24},{18,... | collective-permute-start | bytes 1572872 | tf_op jit(solution)/shard_map/ppermute | solution.py:261
  153.1 36.8 %collective-permute-start.18 = (bf16[2,128,2048]{2,1,0:T(8,128)(2,1)S(1)}, bf16[2,128,2048]{2,1,0:T(8,128)(2,1)S(1)}, u32[]{:S(2)}, u32[]{:S(2)}) collective-permute-start(bf16[2,128,2048]{2,1,0:T(8,128)(2,1)S(1)} %get-tuple-element.34), channel_id=1, source_target_pairs={{0,1},{1,0},{2,3},{3,2},{4,5},{5,4},{6,7},{7,6},{8,9},{9,8},{10,11... | collective-permute-start | bytes 3145736 | tf_op jit(solution)/shard_map/ppermute | solution.py:247
  153.6 35.5 %collective-permute-start.16 = (bf16[128,2048]{1,0:T(8,128)(2,1)S(1)}, bf16[128,2048]{1,0:T(8,128)(2,1)S(1)}, u32[]{:S(2)}, u32[]{:S(2)}) collective-permute-start(bf16[128,2048]{1,0:T(8,128)(2,1)S(1)} %get-tuple-element.42.rest_0_), channel_id=1, source_target_pairs={{0,26},{2,24},{4,30},{6,28},{8,18},{10,16},{12,22},{14,20},{16,10}... | collective-permute-start | bytes 1572872 | tf_op jit(solution)/shard_map/ppermute | solution.py:261
  157.8 36.1 %collective-permute-start.17 = (bf16[128,2048]{1,0:T(8,128)(2,1)S(1)}, bf16[128,2048]{1,0:T(8,128)(2,1)S(1)}, u32[]{:S(2)}, u32[]{:S(2)}) collective-permute-start(bf16[128,2048]{1,0:T(8,128)(2,1)S(1)} %get-tuple-element.41.rest_1_), channel_id=1, source_target_pairs={{0,10},{2,8},{4,14},{6,12},{8,2},{10,0},{12,6},{14,4},{16,26},{18,... | collective-permute-start | bytes 1572872 | tf_op jit(solution)/shard_map/ppermute | solution.py:261
  175.4 19.4 %collective-permute-start.21 = (bf16[3,128,2048]{2,1,0:T(8,128)(2,1)S(1)}, bf16[3,128,2048]{2,1,0:T(8,128)(2,1)S(1)}, u32[]{:S(2)}, u32[]{:S(2)}) collective-permute-start(bf16[3,128,2048]{2,1,0:T(8,128)(2,1)S(1)} %get-tuple-element.36), channel_id=1, source_target_pairs={{0,1},{1,0},{2,3},{3,2},{4,5},{5,4},{6,7},{7,6},{8,9},{9,8},{10,11... | collective-permute-start | bytes 4718600 | tf_op jit(solution)/shard_map/ppermute | solution.py:247
  190.3 41.7 %collective-permute-start.19 = (bf16[128,2048]{1,0:T(8,128)(2,1)S(1)}, bf16[128,2048]{1,0:T(8,128)(2,1)S(1)}, u32[]{:S(2)}, u32[]{:S(2)}) collective-permute-start(bf16[128,2048]{1,0:T(8,128)(2,1)S(1)} %get-tuple-element.40), channel_id=1, source_target_pairs={{0,28},{2,30},{4,24},{6,26},{8,20},{10,22},{12,16},{14,18},{16,12}... | collective-permute-start | bytes 1572872 | tf_op jit(solution)/shard_map/ppermute | solution.py:261
  194.8 38.1 %collective-permute-start.20 = (bf16[128,2048]{1,0:T(8,128)(2,1)S(1)}, bf16[128,2048]{1,0:T(8,128)(2,1)S(1)}, u32[]{:S(2)}, u32[]{:S(2)}) collective-permute-start(bf16[128,2048]{1,0:T(8,128)(2,1)S(1)} %get-tuple-element.39), channel_id=1, source_target_pairs={{0,12},{2,14},{4,8},{6,10},{8,4},{10,6},{12,0},{14,2},{16,28},{18,... | collective-permute-start | bytes 1572872 | tf_op jit(solution)/shard_map/ppermute | solution.py:261
  195.2 57.0 %collective-permute-start.22 = (bf16[128,2048]{1,0:T(8,128)(2,1)S(1)}, bf16[128,2048]{1,0:T(8,128)(2,1)S(1)}, u32[]{:S(2)}, u32[]{:S(2)}) collective-permute-start(bf16[128,2048]{1,0:T(8,128)(2,1)S(1)} %get-tuple-element.38), channel_id=1, source_target_pairs={{0,30},{2,28},{4,26},{6,24},{8,22},{10,20},{12,18},{14,16},{16,14}... | collective-permute-start | bytes 1572872 | tf_op jit(solution)/shard_map/ppermute | solution.py:261
  232.9 22.1 %collective-permute-start.23 = (bf16[128,2048]{1,0:T(8,128)(2,1)S(1)}, bf16[128,2048]{1,0:T(8,128)(2,1)S(1)}, u32[]{:S(2)}, u32[]{:S(2)}) collective-permute-start(bf16[128,2048]{1,0:T(8,128)(2,1)S(1)} %get-tuple-element.37), channel_id=1, source_target_pairs={{0,14},{2,12},{4,10},{6,8},{8,6},{10,4},{12,2},{14,0},{16,30},{18,... | collective-permute-start | bytes 1572872 | tf_op jit(solution)/shard_map/ppermute | solution.py:261
  (4 other events, 5.6 us)

commit v3 on v2

--- a/solution.py
+++ b/solution.py
@@ -224,8 +224,14 @@
 
     half = dp_count // 2
     far, near = list(range(half, dp_count)), list(range(1, half)) + [0]
-    order = far[:1] + [r for pair in zip(far[1:], near) for r in pair] + near[half - 1 :]
-    sizes = [1] + [2] * (half - 2) + [3]
+    groups, at = [far[:1]], 0
+    for k in range(1, half - 1):
+        to = at + (2 if k == 3 else 1)
+        groups.append([far[k]] + near[at:to])
+        at = to
+    groups.append(far[half - 1 :] + near[at:])
+    order = [r for group in groups for r in group]
+    sizes = [len(group) for group in groups]
     partner = jnp.bitwise_xor(me.astype(jnp.int32), jnp.asarray(order, jnp.int32))
     numbers = jnp.arange(block_count, dtype=jnp.int32)
     named = (destination[:, 0][None, :] == partner[:, None]) & (numbers < counts[0])[None, :]

time: 260 us -> 245 us (0.942)
  waiting for transfers between devices: 84.2 us -> 68.8 us
    ppermute x15, waiting for transfers between devices: 81.2 us -> 65.9 us  [per_device(): block = lax.ppermute(block, 'dp', [(i, i ^ r) for i in range(dp_count)])]
  transfers between devices with their start and end apart: 24 -> 24, of which waited for: 9 -> 10; matrix products, arithmetic and copies ran while one was open for 8% -> 8% of each run, Pallas kernels for 38% -> 40%
where the time goes in v3:
time: 245 us; the launch traced here: 243 us
  Pallas kernels  109 us (44%)
  waiting for transfers between devices  68.8 us (28%)
  starting transfers between devices  38 us (16%)
  local copies, waits for them, and re-layouts  18 us (7%)
  other arithmetic  8.28 us (3%)
    pallas_call x8, Pallas kernels, mix_blocks(): pl.pallas_call(functools.partial(mix_kernel, slots, parts, width, len(aft...  109 us
    ppermute x15, waiting for transfers between devices, per_device(): block = lax.ppermute(block, 'dp', [(i, i ^ r) for i in range(dp_count)])  65.9 us
    ppermute x15, starting transfers between devices, per_device(): block = lax.ppermute(block, 'dp', [(i, i ^ r) for i in range(dp_count)])  33.1 us
    dynamic_update_slice x15, local copies, waits for them, and re-layouts, per_device(): lax.dynamic_update_index_in_dim(result, block, jnp.bitwise_xor(me, r), 0)  12.6 us
  transfers between devices with their start and end apart: 24, of which 10 were waited for; matrix products, arithmetic and copies ran while one was open for 8% of the time, Pallas kernels for 40%

profile of v3, /device:TPU:16, one launch (start us, length us, event | category | flops | bytes accessed | tf_op | source)
XLA Modules:
  0.0 242.7 jit_solution(6149638739304805780)
XLA Ops:
  1.8 3.4 %collective-permute-start = (bf16[3,16,2048]{2,1,0:T(8,128)(2,1)S(1)}, bf16[3,16,2048]{2,1,0:T(8,128)(2,1)S(1)}, u32[]{:S(2)}, u32[]{:S(2)}) collective-permute-start(bf16[3,16,2048]{2,1,0:T(8,128)(2,1)S(1)} %pad_maximum_fusion), channel_id=1, source_target_pairs={{0,2},{2,4},{4,6},{6,8},{8,10},{10,12},{12,14},{14,16},{16,18},{18... | collective-permute-start | bytes 589832 | tf_op jit(solution)/shard_map/ppermute | solution.py:216
  9.1 3.0 %collective-permute-done.tails_ref = bf16[3,16,2048]{2,1,0:T(8,128)(2,1)S(1)} collective-permute-done((bf16[3,16,2048]{2,1,0:T(8,128)(2,1)S(1)}, bf16[3,16,2048]{2,1,0:T(8,128)(2,1)S(1)}, u32[]{:S(2)}, u32[]{:S(2)}) %collective-permute-start) | collective-permute-done | bytes 196640 | tf_op jit(solution)/shard_map/ppermute | solution.py:216
  14.8 10.7 %shard_map.101 = (bf16[1,128,2048]{2,1,0:T(8,128)(2,1)S(1)}, bf16[1,128,2048]{2,1,0:T(8,128)(2,1)S(1)}) custom-call(s32[1]{0:T(128)S(1)} %bitcast.73, s32[48]{0:T(128)S(1)} %compare_convert_fusion.clean, s32[12]{0:T(128)S(1)} %convert_reduce_fusion.lead_clean, s32[1]{0:T(128)} %bitcast.3.core, bf16[1536,2048]{1,0:T(8,128)(2,1)} %qp_ref.15, ...), custom_call_target="tpu_custom_call" | custom-call | flops 2147483648 | bytes 23068672 | tf_op jit(solution)/shard_map/pallas_call | solution.py:157
  25.7 13.9 %shard_map.102 = (bf16[2,128,2048]{2,1,0:T(8,128)(2,1)S(1)}, bf16[2,128,2048]{2,1,0:T(8,128)(2,1)}) custom-call(s32[2]{0:T(128)S(1)} %get-tuple-element.55.block_of, s32[48]{0:T(128)S(1)} %compare_convert_fusion.clean, s32[12]{0:T(128)S(1)} %convert_reduce_fusion.lead_clean, s32[1]{0:T(128)} %bitcast.3.core, bf16[1536,2048]{1,0:T(8,128)(2,1)} %qp_ref.15, ...), custom_call_target="tpu_custom_call" | custom-call | flops 4294967296 | bytes 29360128 | tf_op jit(solution)/shard_map/pallas_call | solution.py:157
  41.5 13.0 %shard_map.103 = (bf16[2,128,2048]{2,1,0:T(8,128)(2,1)S(1)}, bf16[2,128,2048]{2,1,0:T(8,128)(2,1)S(1)}) custom-call(s32[2]{0:T(128)S(1)} %get-tuple-element.54.block_of, s32[48]{0:T(128)S(1)} %compare_convert_fusion.clean, s32[12]{0:T(128)S(1)} %convert_reduce_fusion.lead_clean, s32[1]{0:T(128)} %bitcast.3.core, bf16[1536,2048]{1,0:T(8,128)(2,1)} %qp_ref.15, ...), custom_call_target="tpu_custom_call" | custom-call | flops 4294967296 | bytes 29360128 | tf_op jit(solution)/shard_map/pallas_call | solution.py:157
  56.1 2.7 %collective-permute-start.4 = (bf16[128,2048]{1,0:T(8,128)(2,1)S(1)}, bf16[128,2048]{1,0:T(8,128)(2,1)S(1)}, u32[]{:S(2)}, u32[]{:S(2)}) collective-permute-start(bf16[128,2048]{1,0:T(8,128)(2,1)S(1)} %get-tuple-element.49.rest_0_), channel_id=1, source_target_pairs={{0,18},{2,16},{4,22},{6,20},{8,26},{10,24},{12,30},{14,28},{16,2},... | collective-permute-start | bytes 1572872 | tf_op jit(solution)/shard_map/ppermute | solution.py:267
  61.1 16.4 %shard_map.104 = (bf16[3,128,2048]{2,1,0:T(8,128)(2,1)S(1)}, bf16[3,128,2048]{2,1,0:T(8,128)(2,1)S(1)}) custom-call(s32[3]{0:T(128)S(1)} %slice.141.block_of, s32[48]{0:T(128)S(1)} %compare_convert_fusion.clean, s32[12]{0:T(128)S(1)} %convert_reduce_fusion.lead_clean, s32[1]{0:T(128)} %bitcast.3.core, bf16[1536,2048]{1,0:T(8,128)(2,1)} %qp_ref.15, ...), custom_call_target="tpu_custom_call" | custom-call | flops 6442450944 | bytes 35651584 | tf_op jit(solution)/shard_map/pallas_call | solution.py:157
  78.9 2.7 %collective-permute-start.7 = (bf16[128,2048]{1,0:T(8,128)(2,1)S(1)}, bf16[128,2048]{1,0:T(8,128)(2,1)S(1)}, u32[]{:S(2)}, u32[]{:S(2)}) collective-permute-start(bf16[128,2048]{1,0:T(8,128)(2,1)S(1)} %get-tuple-element.47.rest_0_), channel_id=1, source_target_pairs={{0,20},{2,22},{4,16},{6,18},{8,28},{10,30},{12,24},{14,26},{16,4},... | collective-permute-start | bytes 1572872 | tf_op jit(solution)/shard_map/ppermute | solution.py:267
  81.6 2.4 %collective-permute-start.8 = (bf16[128,2048]{1,0:T(8,128)(2,1)S(1)}, bf16[128,2048]{1,0:T(8,128)(2,1)S(1)}, u32[]{:S(2)}, u32[]{:S(2)}) collective-permute-start(bf16[128,2048]{1,0:T(8,128)(2,1)S(1)} %get-tuple-element.46.rest_1_), channel_id=1, source_target_pairs={{0,4},{2,6},{4,0},{6,2},{8,12},{10,14},{12,8},{14,10},{16,20},{18,... | collective-permute-start | bytes 1572872 | tf_op jit(solution)/shard_map/ppermute | solution.py:267
  84.0 13.1 %shard_map.105 = (bf16[2,128,2048]{2,1,0:T(8,128)(2,1)S(1)}, bf16[2,128,2048]{2,1,0:T(8,128)(2,1)S(1)}) custom-call(s32[2]{0:T(128)S(1)} %get-tuple-element.53.block_of, s32[48]{0:T(128)S(1)} %compare_convert_fusion.clean, s32[12]{0:T(128)S(1)} %convert_reduce_fusion.lead_clean, s32[1]{0:T(128)} %bitcast.3.core, bf16[1536,2048]{1,0:T(8,128)(2,1)} %qp_ref.15, ...), custom_call_target="tpu_custom_call" | custom-call | flops 4294967296 | bytes 29360128 | tf_op jit(solution)/shard_map/pallas_call | solution.py:157
  100.3 9.0 %collective-permute-done.7 = bf16[128,2048]{1,0:T(8,128)(2,1)S(1)} collective-permute-done((bf16[128,2048]{1,0:T(8,128)(2,1)S(1)}, bf16[128,2048]{1,0:T(8,128)(2,1)S(1)}, u32[]{:S(2)}, u32[]{:S(2)}) %collective-permute-start.7) | collective-permute-done | bytes 524320 | tf_op jit(solution)/shard_map/ppermute | solution.py:267
  111.6 3.5 %collective-permute-start.10 = (bf16[128,2048]{1,0:T(8,128)(2,1)S(1)}, bf16[128,2048]{1,0:T(8,128)(2,1)S(1)}, u32[]{:S(2)}, u32[]{:S(2)}) collective-permute-start(bf16[128,2048]{1,0:T(8,128)(2,1)S(1)} %get-tuple-element.39.rest_0_), channel_id=1, source_target_pairs={{0,22},{2,20},{4,18},{6,16},{8,30},{10,28},{12,26},{14,24},{16,6},... | collective-permute-start | bytes 1572872 | tf_op jit(solution)/shard_map/ppermute | solution.py:267
  115.1 2.8 %collective-permute-start.11 = (bf16[128,2048]{1,0:T(8,128)(2,1)S(1)}, bf16[128,2048]{1,0:T(8,128)(2,1)S(1)}, u32[]{:S(2)}, u32[]{:S(2)}) collective-permute-start(bf16[128,2048]{1,0:T(8,128)(2,1)S(1)} %get-tuple-element.38.rest_1_), channel_id=1, source_target_pairs={{0,6},{2,4},{4,2},{6,0},{8,14},{10,12},{12,10},{14,8},{16,22},{18,... | collective-permute-start | bytes 1572872 | tf_op jit(solution)/shard_map/ppermute | solution.py:267
  120.7 3.2 %collective-permute-start.15 = (bf16[128,2048]{1,0:T(8,128)(2,1)S(1)}, bf16[128,2048]{1,0:T(8,128)(2,1)S(1)}, u32[]{:S(2)}, u32[]{:S(2)}) collective-permute-start(bf16[128,2048]{1,0:T(8,128)(2,1)S(1)} %get-tuple-element.44.rest_1_), channel_id=1, source_target_pairs={{0,10},{2,8},{4,14},{6,12},{8,2},{10,0},{12,6},{14,4},{16,26},{18,... | collective-permute-start | bytes 1572872 | tf_op jit(solution)/shard_map/ppermute | solution.py:267
  123.9 13.4 %shard_map.106 = (bf16[2,128,2048]{2,1,0:T(8,128)(2,1)S(1)}, bf16[2,128,2048]{2,1,0:T(8,128)(2,1)S(1)}) custom-call(s32[2]{0:T(128)S(1)} %get-tuple-element.52.block_of, s32[48]{0:T(128)S(1)} %compare_convert_fusion.clean, s32[12]{0:T(128)S(1)} %convert_reduce_fusion.lead_clean, s32[1]{0:T(128)} %bitcast.3.core, bf16[1536,2048]{1,0:T(8,128)(2,1)} %qp_ref.15, ...), custom_call_target="tpu_custom_call" | custom-call | flops 4294967296 | bytes 29360128 | tf_op jit(solution)/shard_map/pallas_call | solution.py:157
  137.3 13.4 %shard_map.107 = (bf16[2,128,2048]{2,1,0:T(8,128)(2,1)S(1)}, bf16[2,128,2048]{2,1,0:T(8,128)(2,1)S(1)}) custom-call(s32[2]{0:T(128)S(1)} %get-tuple-element.51.block_of, s32[48]{0:T(128)S(1)} %compare_convert_fusion.clean, s32[12]{0:T(128)S(1)} %convert_reduce_fusion.lead_clean, s32[1]{0:T(128)} %bitcast.3.core, bf16[1536,2048]{1,0:T(8,128)(2,1)} %qp_ref.15, ...), custom_call_target="tpu_custom_call" | custom-call | flops 4294967296 | bytes 29360128 | tf_op jit(solution)/shard_map/pallas_call | solution.py:157
  153.9 6.8 %collective-permute-done.14 = bf16[128,2048]{1,0:T(8,128)(2,1)S(1)} collective-permute-done((bf16[128,2048]{1,0:T(8,128)(2,1)S(1)}, bf16[128,2048]{1,0:T(8,128)(2,1)S(1)}, u32[]{:S(2)}, u32[]{:S(2)}) %collective-permute-start.14) | collective-permute-done | bytes 524320 | tf_op jit(solution)/shard_map/ppermute | solution.py:267
  163.9 2.6 %collective-permute-start.17 = (bf16[128,2048]{1,0:T(8,128)(2,1)S(1)}, bf16[128,2048]{1,0:T(8,128)(2,1)S(1)}, u32[]{:S(2)}, u32[]{:S(2)}) collective-permute-start(bf16[128,2048]{1,0:T(8,128)(2,1)S(1)} %get-tuple-element.43.rest_0_), channel_id=1, source_target_pairs={{0,26},{2,24},{4,30},{6,28},{8,18},{10,16},{12,22},{14,20},{16,10}... | collective-permute-start | bytes 1572872 | tf_op jit(solution)/shard_map/ppermute | solution.py:267
  166.5 3.7 %collective-permute-start.18 = (bf16[128,2048]{1,0:T(8,128)(2,1)S(1)}, bf16[128,2048]{1,0:T(8,128)(2,1)S(1)}, u32[]{:S(2)}, u32[]{:S(2)}) collective-permute-start(bf16[128,2048]{1,0:T(8,128)(2,1)S(1)} %get-tuple-element.42.rest_1_), channel_id=1, source_target_pairs={{0,12},{2,14},{4,8},{6,10},{8,4},{10,6},{12,0},{14,2},{16,28},{18,... | collective-permute-start | bytes 1572872 | tf_op jit(solution)/shard_map/ppermute | solution.py:267
  170.2 14.7 %shard_map.108 = (bf16[2,128,2048]{2,1,0:T(8,128)(2,1)S(1)}, bf16[2,128,2048]{2,1,0:T(8,128)(2,1)S(1)}) custom-call(s32[2]{0:T(128)S(1)} %get-tuple-element.50.block_of, s32[48]{0:T(128)S(1)} %compare_convert_fusion.clean, s32[12]{0:T(128)S(1)} %convert_reduce_fusion.lead_clean, s32[1]{0:T(128)} %bitcast.3.core, bf16[1536,2048]{1,0:T(8,128)(2,1)} %qp_ref.15, ...), custom_call_target="tpu_custom_call" | custom-call | flops 4294967296 | bytes 29360128 | tf_op jit(solution)/shard_map/pallas_call | solution.py:157
  186.9 4.5 %collective-permute-done.17 = bf16[128,2048]{1,0:T(8,128)(2,1)S(1)} collective-permute-done((bf16[128,2048]{1,0:T(8,128)(2,1)S(1)}, bf16[128,2048]{1,0:T(8,128)(2,1)S(1)}, u32[]{:S(2)}, u32[]{:S(2)}) %collective-permute-start.17) | collective-permute-done | bytes 524320 | tf_op jit(solution)/shard_map/ppermute | solution.py:267
  195.2 3.2 %collective-permute-start.23 = (bf16[128,2048]{1,0:T(8,128)(2,1)S(1)}, bf16[128,2048]{1,0:T(8,128)(2,1)S(1)}, u32[]{:S(2)}, u32[]{:S(2)}) collective-permute-start(bf16[128,2048]{1,0:T(8,128)(2,1)S(1)} %fusion.14), channel_id=1, source_target_pairs={{0,30},{2,28},{4,26},{6,24},{8,22},{10,20},{12,18},{14,16},{16,14}... | collective-permute-start | bytes 1572872 | tf_op jit(solution)/shard_map/ppermute | solution.py:267
  198.4 22.3 %collective-permute-done.20 = bf16[128,2048]{1,0:T(8,128)(2,1)S(1)} collective-permute-done((bf16[128,2048]{1,0:T(8,128)(2,1)S(1)}, bf16[128,2048]{1,0:T(8,128)(2,1)S(1)}, u32[]{:S(2)}, u32[]{:S(2)}) %collective-permute-start.20) | collective-permute-done | bytes 524320 | tf_op jit(solution)/shard_map/ppermute | solution.py:267
  224.3 16.7 %collective-permute-done.23 = bf16[128,2048]{1,0:T(8,128)(2,1)S(1)} collective-permute-done((bf16[128,2048]{1,0:T(8,128)(2,1)S(1)}, bf16[128,2048]{1,0:T(8,128)(2,1)S(1)}, u32[]{:S(2)}, u32[]{:S(2)}) %collective-permute-start.23) | collective-permute-done | bytes 524320 | tf_op jit(solution)/shard_map/ppermute | solution.py:267
  (78 shorter events, 40.5 us)
Async XLA Ops:
  1.8 10.3 %collective-permute-start = (bf16[3,16,2048]{2,1,0:T(8,128)(2,1)S(1)}, bf16[3,16,2048]{2,1,0:T(8,128)(2,1)S(1)}, u32[]{:S(2)}, u32[]{:S(2)}) collective-permute-start(bf16[3,16,2048]{2,1,0:T(8,128)(2,1)S(1)} %pad_maximum_fusion), channel_id=1, source_target_pairs={{0,2},{2,4},{4,6},{6,8},{8,10},{10,12},{12,14},{14,16},{16,18},{18... | collective-permute-start | bytes 589832 | tf_op jit(solution)/shard_map/ppermute | solution.py:216
  25.6 14.6 %collective-permute-start.1 = (bf16[1,128,2048]{2,1,0:T(8,128)(2,1)S(1)}, bf16[1,128,2048]{2,1,0:T(8,128)(2,1)}, u32[]{:S(2)}, u32[]{:S(2)}) collective-permute-start(bf16[1,128,2048]{2,1,0:T(8,128)(2,1)S(1)} %get-tuple-element.22), channel_id=1, source_target_pairs={{0,1},{1,0},{2,3},{3,2},{4,5},{5,4},{6,7},{7,6},{8,9},{9,8},{10,11... | collective-permute-start | bytes 1572872 | tf_op jit(solution)/shard_map/ppermute | solution.py:253
  39.6 15.1 %collective-permute-start.3 = (bf16[2,128,2048]{2,1,0:T(8,128)(2,1)}, bf16[2,128,2048]{2,1,0:T(8,128)(2,1)}, u32[]{:S(2)}, u32[]{:S(2)}) collective-permute-start(bf16[2,128,2048]{2,1,0:T(8,128)(2,1)} %get-tuple-element.24), channel_id=1, source_target_pairs={{0,1},{1,0},{2,3},{3,2},{4,5},{5,4},{6,7},{7,6},{8,9},{9,8},{10,11... | collective-permute-start | bytes 3145736 | tf_op jit(solution)/shard_map/ppermute | solution.py:253
  41.4 36.3 %collective-permute-start.2 = (bf16[128,2048]{1,0:T(8,128)(2,1)S(1)}, bf16[128,2048]{1,0:T(8,128)(2,1)S(1)}, u32[]{:S(2)}, u32[]{:S(2)}) collective-permute-start(bf16[128,2048]{1,0:T(8,128)(2,1)S(1)} %fusion.rest_0_), channel_id=1, source_target_pairs={{0,16},{2,18},{4,20},{6,22},{8,24},{10,26},{12,28},{14,30},{16,0},... | collective-permute-start | bytes 1572872 | tf_op jit(solution)/shard_map/ppermute | solution.py:267
  54.5 24.0 %collective-permute-start.6 = (bf16[2,128,2048]{2,1,0:T(8,128)(2,1)S(1)}, bf16[2,128,2048]{2,1,0:T(8,128)(2,1)S(1)}, u32[]{:S(2)}, u32[]{:S(2)}) collective-permute-start(bf16[2,128,2048]{2,1,0:T(8,128)(2,1)S(1)} %get-tuple-element.26), channel_id=1, source_target_pairs={{0,1},{1,0},{2,3},{3,2},{4,5},{5,4},{6,7},{7,6},{8,9},{9,8},{10,11... | collective-permute-start | bytes 3145736 | tf_op jit(solution)/shard_map/ppermute | solution.py:253
  56.1 42.6 %collective-permute-start.4 = (bf16[128,2048]{1,0:T(8,128)(2,1)S(1)}, bf16[128,2048]{1,0:T(8,128)(2,1)S(1)}, u32[]{:S(2)}, u32[]{:S(2)}) collective-permute-start(bf16[128,2048]{1,0:T(8,128)(2,1)S(1)} %get-tuple-element.49.rest_0_), channel_id=1, source_target_pairs={{0,18},{2,16},{4,22},{6,20},{8,26},{10,24},{12,30},{14,28},{16,2},... | collective-permute-start | bytes 1572872 | tf_op jit(solution)/shard_map/ppermute | solution.py:267
  58.8 40.7 %collective-permute-start.5 = (bf16[128,2048]{1,0:T(8,128)(2,1)S(1)}, bf16[128,2048]{1,0:T(8,128)(2,1)S(1)}, u32[]{:S(2)}, u32[]{:S(2)}) collective-permute-start(bf16[128,2048]{1,0:T(8,128)(2,1)S(1)} %get-tuple-element.48.rest_1_), channel_id=1, source_target_pairs={{0,2},{2,0},{4,6},{6,4},{8,10},{10,8},{12,14},{14,12},{16,18},{18,... | collective-permute-start | bytes 1572872 | tf_op jit(solution)/shard_map/ppermute | solution.py:267
  77.6 33.5 %collective-permute-start.9 = (bf16[3,128,2048]{2,1,0:T(8,128)(2,1)S(1)}, bf16[3,128,2048]{2,1,0:T(8,128)(2,1)S(1)}, u32[]{:S(2)}, u32[]{:S(2)}) collective-permute-start(bf16[3,128,2048]{2,1,0:T(8,128)(2,1)S(1)} %get-tuple-element.28), channel_id=1, source_target_pairs={{0,1},{1,0},{2,3},{3,2},{4,5},{5,4},{6,7},{7,6},{8,9},{9,8},{10,11... | collective-permute-start | bytes 4718600 | tf_op jit(solution)/shard_map/ppermute | solution.py:253
  78.9 30.4 %collective-permute-start.7 = (bf16[128,2048]{1,0:T(8,128)(2,1)S(1)}, bf16[128,2048]{1,0:T(8,128)(2,1)S(1)}, u32[]{:S(2)}, u32[]{:S(2)}) collective-permute-start(bf16[128,2048]{1,0:T(8,128)(2,1)S(1)} %get-tuple-element.47.rest_0_), channel_id=1, source_target_pairs={{0,20},{2,22},{4,16},{6,18},{8,28},{10,30},{12,24},{14,26},{16,4},... | collective-permute-start | bytes 1572872 | tf_op jit(solution)/shard_map/ppermute | solution.py:267
  81.6 28.6 %collective-permute-start.8 = (bf16[128,2048]{1,0:T(8,128)(2,1)S(1)}, bf16[128,2048]{1,0:T(8,128)(2,1)S(1)}, u32[]{:S(2)}, u32[]{:S(2)}) collective-permute-start(bf16[128,2048]{1,0:T(8,128)(2,1)S(1)} %get-tuple-element.46.rest_1_), channel_id=1, source_target_pairs={{0,4},{2,6},{4,0},{6,2},{8,12},{10,14},{12,8},{14,10},{16,20},{18,... | collective-permute-start | bytes 1572872 | tf_op jit(solution)/shard_map/ppermute | solution.py:267
  98.6 19.5 %collective-permute-start.13 = (bf16[2,128,2048]{2,1,0:T(8,128)(2,1)S(1)}, bf16[2,128,2048]{2,1,0:T(8,128)(2,1)S(1)}, u32[]{:S(2)}, u32[]{:S(2)}) collective-permute-start(bf16[2,128,2048]{2,1,0:T(8,128)(2,1)S(1)} %get-tuple-element.30), channel_id=1, source_target_pairs={{0,1},{1,0},{2,3},{3,2},{4,5},{5,4},{6,7},{7,6},{8,9},{9,8},{10,11... | collective-permute-start | bytes 3145736 | tf_op jit(solution)/shard_map/ppermute | solution.py:253
  111.6 39.1 %collective-permute-start.10 = (bf16[128,2048]{1,0:T(8,128)(2,1)S(1)}, bf16[128,2048]{1,0:T(8,128)(2,1)S(1)}, u32[]{:S(2)}, u32[]{:S(2)}) collective-permute-start(bf16[128,2048]{1,0:T(8,128)(2,1)S(1)} %get-tuple-element.39.rest_0_), channel_id=1, source_target_pairs={{0,22},{2,20},{4,18},{6,16},{8,30},{10,28},{12,26},{14,24},{16,6},... | collective-permute-start | bytes 1572872 | tf_op jit(solution)/shard_map/ppermute | solution.py:267
  115.1 36.6 %collective-permute-start.11 = (bf16[128,2048]{1,0:T(8,128)(2,1)S(1)}, bf16[128,2048]{1,0:T(8,128)(2,1)S(1)}, u32[]{:S(2)}, u32[]{:S(2)}) collective-permute-start(bf16[128,2048]{1,0:T(8,128)(2,1)S(1)} %get-tuple-element.38.rest_1_), channel_id=1, source_target_pairs={{0,6},{2,4},{4,2},{6,0},{8,14},{10,12},{12,10},{14,8},{16,22},{18,... | collective-permute-start | bytes 1572872 | tf_op jit(solution)/shard_map/ppermute | solution.py:267
  117.9 35.1 %collective-permute-start.12 = (bf16[128,2048]{1,0:T(8,128)(2,1)S(1)}, bf16[128,2048]{1,0:T(8,128)(2,1)S(1)}, u32[]{:S(2)}, u32[]{:S(2)}) collective-permute-start(bf16[128,2048]{1,0:T(8,128)(2,1)S(1)} %get-tuple-element.37.rest_2_), channel_id=1, source_target_pairs={{0,8},{2,10},{4,12},{6,14},{8,0},{10,2},{12,4},{14,6},{16,24},{18,... | collective-permute-start | bytes 1572872 | tf_op jit(solution)/shard_map/ppermute | solution.py:267
  118.5 42.2 %collective-permute-start.14 = (bf16[128,2048]{1,0:T(8,128)(2,1)S(1)}, bf16[128,2048]{1,0:T(8,128)(2,1)S(1)}, u32[]{:S(2)}, u32[]{:S(2)}) collective-permute-start(bf16[128,2048]{1,0:T(8,128)(2,1)S(1)} %get-tuple-element.45.rest_0_), channel_id=1, source_target_pairs={{0,24},{2,26},{4,28},{6,30},{8,16},{10,18},{12,20},{14,22},{16,8},... | collective-permute-start | bytes 1572872 | tf_op jit(solution)/shard_map/ppermute | solution.py:267
  120.7 41.9 %collective-permute-start.15 = (bf16[128,2048]{1,0:T(8,128)(2,1)S(1)}, bf16[128,2048]{1,0:T(8,128)(2,1)S(1)}, u32[]{:S(2)}, u32[]{:S(2)}) collective-permute-start(bf16[128,2048]{1,0:T(8,128)(2,1)S(1)} %get-tuple-element.44.rest_1_), channel_id=1, source_target_pairs={{0,10},{2,8},{4,14},{6,12},{8,2},{10,0},{12,6},{14,4},{16,26},{18,... | collective-permute-start | bytes 1572872 | tf_op jit(solution)/shard_map/ppermute | solution.py:267
  150.8 12.7 %collective-permute-start.16 = (bf16[2,128,2048]{2,1,0:T(8,128)(2,1)S(1)}, bf16[2,128,2048]{2,1,0:T(8,128)(2,1)S(1)}, u32[]{:S(2)}, u32[]{:S(2)}) collective-permute-start(bf16[2,128,2048]{2,1,0:T(8,128)(2,1)S(1)} %get-tuple-element.32), channel_id=1, source_target_pairs={{0,1},{1,0},{2,3},{3,2},{4,5},{5,4},{6,7},{7,6},{8,9},{9,8},{10,11... | collective-permute-start | bytes 3145736 | tf_op jit(solution)/shard_map/ppermute | solution.py:253
  151.7 33.2 %collective-permute-start.19 = (bf16[2,128,2048]{2,1,0:T(8,128)(2,1)S(1)}, bf16[2,128,2048]{2,1,0:T(8,128)(2,1)S(1)}, u32[]{:S(2)}, u32[]{:S(2)}) collective-permute-start(bf16[2,128,2048]{2,1,0:T(8,128)(2,1)S(1)} %get-tuple-element.34), channel_id=1, source_target_pairs={{0,1},{1,0},{2,3},{3,2},{4,5},{5,4},{6,7},{7,6},{8,9},{9,8},{10,11... | collective-permute-start | bytes 3145736 | tf_op jit(solution)/shard_map/ppermute | solution.py:253
  163.9 27.5 %collective-permute-start.17 = (bf16[128,2048]{1,0:T(8,128)(2,1)S(1)}, bf16[128,2048]{1,0:T(8,128)(2,1)S(1)}, u32[]{:S(2)}, u32[]{:S(2)}) collective-permute-start(bf16[128,2048]{1,0:T(8,128)(2,1)S(1)} %get-tuple-element.43.rest_0_), channel_id=1, source_target_pairs={{0,26},{2,24},{4,30},{6,28},{8,18},{10,16},{12,22},{14,20},{16,10}... | collective-permute-start | bytes 1572872 | tf_op jit(solution)/shard_map/ppermute | solution.py:267
  166.5 27.8 %collective-permute-start.18 = (bf16[128,2048]{1,0:T(8,128)(2,1)S(1)}, bf16[128,2048]{1,0:T(8,128)(2,1)S(1)}, u32[]{:S(2)}, u32[]{:S(2)}) collective-permute-start(bf16[128,2048]{1,0:T(8,128)(2,1)S(1)} %get-tuple-element.42.rest_1_), channel_id=1, source_target_pairs={{0,12},{2,14},{4,8},{6,10},{8,4},{10,6},{12,0},{14,2},{16,28},{18,... | collective-permute-start | bytes 1572872 | tf_op jit(solution)/shard_map/ppermute | solution.py:267
  184.8 10.3 %collective-permute-start.22 = (bf16[2,128,2048]{2,1,0:T(8,128)(2,1)S(1)}, bf16[2,128,2048]{2,1,0:T(8,128)(2,1)S(1)}, u32[]{:S(2)}, u32[]{:S(2)}) collective-permute-start(bf16[2,128,2048]{2,1,0:T(8,128)(2,1)S(1)} %get-tuple-element.36), channel_id=1, source_target_pairs={{0,1},{1,0},{2,3},{3,2},{4,5},{5,4},{6,7},{7,6},{8,9},{9,8},{10,11... | collective-permute-start | bytes 3145736 | tf_op jit(solution)/shard_map/ppermute | solution.py:253
  185.3 35.4 %collective-permute-start.20 = (bf16[128,2048]{1,0:T(8,128)(2,1)S(1)}, bf16[128,2048]{1,0:T(8,128)(2,1)S(1)}, u32[]{:S(2)}, u32[]{:S(2)}) collective-permute-start(bf16[128,2048]{1,0:T(8,128)(2,1)S(1)} %get-tuple-element.41), channel_id=1, source_target_pairs={{0,28},{2,30},{4,24},{6,26},{8,20},{10,22},{12,16},{14,18},{16,12}... | collective-permute-start | bytes 1572872 | tf_op jit(solution)/shard_map/ppermute | solution.py:267
  186.8 36.6 %collective-permute-start.21 = (bf16[128,2048]{1,0:T(8,128)(2,1)S(1)}, bf16[128,2048]{1,0:T(8,128)(2,1)S(1)}, u32[]{:S(2)}, u32[]{:S(2)}) collective-permute-start(bf16[128,2048]{1,0:T(8,128)(2,1)S(1)} %get-tuple-element.40), channel_id=1, source_target_pairs={{0,14},{2,12},{4,10},{6,8},{8,6},{10,4},{12,2},{14,0},{16,30},{18,... | collective-permute-start | bytes 1572872 | tf_op jit(solution)/shard_map/ppermute | solution.py:267
  195.2 45.7 %collective-permute-start.23 = (bf16[128,2048]{1,0:T(8,128)(2,1)S(1)}, bf16[128,2048]{1,0:T(8,128)(2,1)S(1)}, u32[]{:S(2)}, u32[]{:S(2)}) collective-permute-start(bf16[128,2048]{1,0:T(8,128)(2,1)S(1)} %fusion.14), channel_id=1, source_target_pairs={{0,30},{2,28},{4,26},{6,24},{8,22},{10,20},{12,18},{14,16},{16,14}... | collective-permute-start | bytes 1572872 | tf_op jit(solution)/shard_map/ppermute | solution.py:267
  (4 other events, 5.6 us)

commit v4 on v3

--- a/solution.py
+++ b/solution.py
@@ -229,7 +229,8 @@
         to = at + (2 if k == 3 else 1)
         groups.append([far[k]] + near[at:to])
         at = to
-    groups.append(far[half - 1 :] + near[at:])
+    groups[-1] += near[at:]
+    groups.append(far[half - 1 :])
     order = [r for group in groups for r in group]
     sizes = [len(group) for group in groups]
     partner = jnp.bitwise_xor(me.astype(jnp.int32), jnp.asarray(order, jnp.int32))

time: 245 us -> 253 us (1.033)
  waiting for transfers between devices: 68.8 us -> 80.3 us
  Pallas kernels: 109 us -> 118 us
  starting transfers between devices: 38 us -> 32 us
  other arithmetic: 8.28 us -> 4.15 us
  local copies, waits for them, and re-layouts: 18 us -> 15.3 us
    ppermute x15, waiting for transfers between devices: 65.9 us -> 75.3 us  [per_device(): block = lax.ppermute(block, 'dp', [(i, i ^ r) for i in range(dp_count)])]
    pallas_call x8, Pallas kernels: 109 us -> 118 us  [mix_blocks(): pl.pallas_call(functools.partial(mix_kernel, slots, parts, width, len(aft...]
    ppermute x15, starting transfers between devices: 33.1 us -> 27.2 us  [per_device(): block = lax.ppermute(block, 'dp', [(i, i ^ r) for i in range(dp_count)])]
  transfers between devices with their start and end apart: 24 -> 24, of which waited for: 10 -> 7; matrix products, arithmetic and copies ran while one was open for 8% -> 7% of each run, Pallas kernels for 40% -> 43%
where the time goes in v4:
time: 253 us; the launch traced here: 251 us
  Pallas kernels  118 us (47%)
  waiting for transfers between devices  80.3 us (32%)
  starting transfers between devices  32 us (13%)
  local copies, waits for them, and re-layouts  15.3 us (6%)
  other arithmetic  4.15 us (2%)
    pallas_call x8, Pallas kernels, mix_blocks(): pl.pallas_call(functools.partial(mix_kernel, slots, parts, width, len(aft...  118 us
    ppermute x15, waiting for transfers between devices, per_device(): block = lax.ppermute(block, 'dp', [(i, i ^ r) for i in range(dp_count)])  75.3 us
    ppermute x15, starting transfers between devices, per_device(): block = lax.ppermute(block, 'dp', [(i, i ^ r) for i in range(dp_count)])  27.2 us
    dynamic_update_slice x15, local copies, waits for them, and re-layouts, per_device(): lax.dynamic_update_index_in_dim(result, block, jnp.bitwise_xor(me, r), 0)  12.4 us
  transfers between devices with their start and end apart: 24, of which 7 were waited for; matrix products, arithmetic and copies ran while one was open for 7% of the time, Pallas kernels for 43%

profile of v4, /device:TPU:16, one launch (start us, length us, event | category | flops | bytes accessed | tf_op | source)
XLA Modules:
  0.0 250.7 jit_solution(15145927232390946761)
XLA Ops:
  1.9 3.4 %collective-permute-start = (bf16[3,16,2048]{2,1,0:T(8,128)(2,1)S(1)}, bf16[3,16,2048]{2,1,0:T(8,128)(2,1)S(1)}, u32[]{:S(2)}, u32[]{:S(2)}) collective-permute-start(bf16[3,16,2048]{2,1,0:T(8,128)(2,1)S(1)} %pad_maximum_fusion), channel_id=1, source_target_pairs={{0,2},{2,4},{4,6},{6,8},{8,10},{10,12},{12,14},{14,16},{16,18},{18... | collective-permute-start | bytes 589832 | tf_op jit(solution)/shard_map/ppermute | solution.py:216
  7.2 5.0 %collective-permute-done.tails_ref = bf16[3,16,2048]{2,1,0:T(8,128)(2,1)S(1)} collective-permute-done((bf16[3,16,2048]{2,1,0:T(8,128)(2,1)S(1)}, bf16[3,16,2048]{2,1,0:T(8,128)(2,1)S(1)}, u32[]{:S(2)}, u32[]{:S(2)}) %collective-permute-start) | collective-permute-done | bytes 196640 | tf_op jit(solution)/shard_map/ppermute | solution.py:216
  12.5 11.2 %shard_map.101 = (bf16[1,128,2048]{2,1,0:T(8,128)(2,1)S(1)}, bf16[1,128,2048]{2,1,0:T(8,128)(2,1)S(1)}) custom-call(s32[1]{0:T(128)} %get-tuple-element.51.block_of, s32[48]{0:T(128)S(1)} %compare_convert_fusion.clean, s32[12]{0:T(128)S(1)} %convert_reduce_fusion.lead_clean, s32[1]{0:T(128)} %bitcast.3.core, bf16[1536,2048]{1,0:T(8,128)(2,1)} %qp_ref.15, ...), custom_call_target="tpu_custom_call" | custom-call | flops 2147483648 | bytes 23068672 | tf_op jit(solution)/shard_map/pallas_call | solution.py:157
  23.8 14.7 %shard_map.102 = (bf16[2,128,2048]{2,1,0:T(8,128)(2,1)S(1)}, bf16[2,128,2048]{2,1,0:T(8,128)(2,1)S(1)}) custom-call(s32[2]{0:T(128)S(1)} %get-tuple-element.57.block_of, s32[48]{0:T(128)S(1)} %compare_convert_fusion.clean, s32[12]{0:T(128)S(1)} %convert_reduce_fusion.lead_clean, s32[1]{0:T(128)} %bitcast.3.core, bf16[1536,2048]{1,0:T(8,128)(2,1)} %qp_ref.15, ...), custom_call_target="tpu_custom_call" | custom-call | flops 4294967296 | bytes 29360128 | tf_op jit(solution)/shard_map/pallas_call | solution.py:157
  39.4 13.0 %shard_map.103 = (bf16[2,128,2048]{2,1,0:T(8,128)(2,1)S(1)}, bf16[2,128,2048]{2,1,0:T(8,128)(2,1)S(1)}) custom-call(s32[2]{0:T(128)S(1)} %get-tuple-element.56.block_of, s32[48]{0:T(128)S(1)} %compare_convert_fusion.clean, s32[12]{0:T(128)S(1)} %convert_reduce_fusion.lead_clean, s32[1]{0:T(128)} %bitcast.3.core, bf16[1536,2048]{1,0:T(8,128)(2,1)} %qp_ref.15, ...), custom_call_target="tpu_custom_call" | custom-call | flops 4294967296 | bytes 29360128 | tf_op jit(solution)/shard_map/pallas_call | solution.py:157
  52.9 1.1 collective-permute-start.4
  54.0 4.0 %collective-permute-start.5 = (bf16[128,2048]{1,0:T(8,128)(2,1)S(1)}, bf16[128,2048]{1,0:T(8,128)(2,1)S(1)}, u32[]{:S(2)}, u32[]{:S(2)}) collective-permute-start(bf16[128,2048]{1,0:T(8,128)(2,1)S(1)} %get-tuple-element.48.rest_1_), channel_id=1, source_target_pairs={{0,2},{2,0},{4,6},{6,4},{8,10},{10,8},{12,14},{14,12},{16,18},{18,... | collective-permute-start | bytes 1572872 | tf_op jit(solution)/shard_map/ppermute | solution.py:268
  58.0 20.8 %shard_map.104 = (bf16[3,128,2048]{2,1,0:T(8,128)(2,1)S(1)}, bf16[3,128,2048]{2,1,0:T(8,128)(2,1)S(1)}) custom-call(s32[3]{0:T(128)S(1)} %get-tuple-element.53.block_of, s32[48]{0:T(128)S(1)} %compare_convert_fusion.clean, s32[12]{0:T(128)S(1)} %convert_reduce_fusion.lead_clean, s32[1]{0:T(128)} %bitcast.3.core, bf16[1536,2048]{1,0:T(8,128)(2,1)} %qp_ref.15, ...), custom_call_target="tpu_custom_call" | custom-call | flops 6442450944 | bytes 35651584 | tf_op jit(solution)/shard_map/pallas_call | solution.py:157
  80.7 13.6 %shard_map.105 = (bf16[2,128,2048]{2,1,0:T(8,128)(2,1)S(1)}, bf16[2,128,2048]{2,1,0:T(8,128)(2,1)S(1)}) custom-call(s32[2]{0:T(128)S(1)} %get-tuple-element.55.block_of, s32[48]{0:T(128)S(1)} %compare_convert_fusion.clean, s32[12]{0:T(128)S(1)} %convert_reduce_fusion.lead_clean, s32[1]{0:T(128)} %bitcast.3.core, bf16[1536,2048]{1,0:T(8,128)(2,1)} %qp_ref.15, ...), custom_call_target="tpu_custom_call" | custom-call | flops 4294967296 | bytes 29360128 | tf_op jit(solution)/shard_map/pallas_call | solution.py:157
  97.0 9.5 %collective-permute-done.7 = bf16[128,2048]{1,0:T(8,128)(2,1)S(1)} collective-permute-done((bf16[128,2048]{1,0:T(8,128)(2,1)S(1)}, bf16[128,2048]{1,0:T(8,128)(2,1)S(1)}, u32[]{:S(2)}, u32[]{:S(2)}) %collective-permute-start.7) | collective-permute-done | bytes 524320 | tf_op jit(solution)/shard_map/ppermute | solution.py:268
  108.8 2.4 collective-permute-start.10
  111.2 3.1 %collective-permute-start.11 = (bf16[128,2048]{1,0:T(8,128)(2,1)S(1)}, bf16[128,2048]{1,0:T(8,128)(2,1)S(1)}, u32[]{:S(2)}, u32[]{:S(2)}) collective-permute-start(bf16[128,2048]{1,0:T(8,128)(2,1)S(1)} %get-tuple-element.40.rest_1_), channel_id=1, source_target_pairs={{0,6},{2,4},{4,2},{6,0},{8,14},{10,12},{12,10},{14,8},{16,22},{18,... | collective-permute-start | bytes 1572872 | tf_op jit(solution)/shard_map/ppermute | solution.py:268
  114.8 2.7 %collective-permute-start.14 = (bf16[128,2048]{1,0:T(8,128)(2,1)S(1)}, bf16[128,2048]{1,0:T(8,128)(2,1)S(1)}, u32[]{:S(2)}, u32[]{:S(2)}) collective-permute-start(bf16[128,2048]{1,0:T(8,128)(2,1)S(1)} %get-tuple-element.45.rest_0_), channel_id=1, source_target_pairs={{0,24},{2,26},{4,28},{6,30},{8,16},{10,18},{12,20},{14,22},{16,8},... | collective-permute-start | bytes 1572872 | tf_op jit(solution)/shard_map/ppermute | solution.py:268
  117.4 2.4 collective-permute-start.15
  119.9 20.2 %shard_map.107 = (bf16[3,128,2048]{2,1,0:T(8,128)(2,1)S(1)}, bf16[3,128,2048]{2,1,0:T(8,128)(2,1)S(1)}) custom-call(s32[3]{0:T(128)S(1)} %get-tuple-element.52.block_of, s32[48]{0:T(128)S(1)} %compare_convert_fusion.clean, s32[12]{0:T(128)S(1)} %convert_reduce_fusion.lead_clean, s32[1]{0:T(128)} %bitcast.3.core, bf16[1536,2048]{1,0:T(8,128)(2,1)} %qp_ref.15, ...), custom_call_target="tpu_custom_call" | custom-call | flops 6442450944 | bytes 35651584 | tf_op jit(solution)/shard_map/pallas_call | solution.py:157
  140.1 13.0 %shard_map.106 = (bf16[2,128,2048]{2,1,0:T(8,128)(2,1)S(1)}, bf16[2,128,2048]{2,1,0:T(8,128)(2,1)S(1)}) custom-call(s32[2]{0:T(128)S(1)} %get-tuple-element.54.block_of, s32[48]{0:T(128)S(1)} %compare_convert_fusion.clean, s32[12]{0:T(128)S(1)} %convert_reduce_fusion.lead_clean, s32[1]{0:T(128)} %bitcast.3.core, bf16[1536,2048]{1,0:T(8,128)(2,1)} %qp_ref.15, ...), custom_call_target="tpu_custom_call" | custom-call | flops 4294967296 | bytes 29360128 | tf_op jit(solution)/shard_map/pallas_call | solution.py:157
  156.2 1.4 collective-permute-done.14
  158.8 11.3 %shard_map.108 = (bf16[1,128,2048]{2,1,0:T(8,128)(2,1)S(1)}, bf16[1,128,2048]{2,1,0:T(8,128)(2,1)S(1)}) custom-call(s32[1]{0:T(128)} %get-tuple-element.50.block_of, s32[48]{0:T(128)S(1)} %compare_convert_fusion.clean, s32[12]{0:T(128)S(1)} %convert_reduce_fusion.lead_clean, s32[1]{0:T(128)} %bitcast.3.core, bf16[1536,2048]{1,0:T(8,128)(2,1)} %qp_ref.15, ...), custom_call_target="tpu_custom_call" | custom-call | flops 2147483648 | bytes 23068672 | tf_op jit(solution)/shard_map/pallas_call | solution.py:157
  171.0 3.0 %collective-permute-start.17 = (bf16[128,2048]{1,0:T(8,128)(2,1)S(1)}, bf16[128,2048]{1,0:T(8,128)(2,1)S(1)}, u32[]{:S(2)}, u32[]{:S(2)}) collective-permute-start(bf16[128,2048]{1,0:T(8,128)(2,1)S(1)} %get-tuple-element.43.rest_0_), channel_id=1, source_target_pairs={{0,26},{2,24},{4,30},{6,28},{8,18},{10,16},{12,22},{14,20},{16,10}... | collective-permute-start | bytes 1572872 | tf_op jit(solution)/shard_map/ppermute | solution.py:268
  175.1 4.5 %collective-permute-start.21 = (bf16[128,2048]{1,0:T(8,128)(2,1)S(1)}, bf16[128,2048]{1,0:T(8,128)(2,1)S(1)}, u32[]{:S(2)}, u32[]{:S(2)}) collective-permute-start(bf16[128,2048]{1,0:T(8,128)(2,1)S(1)} %get-tuple-element.37), channel_id=1, source_target_pairs={{0,14},{2,12},{4,10},{6,8},{8,6},{10,4},{12,2},{14,0},{16,30},{18,... | collective-permute-start | bytes 1572872 | tf_op jit(solution)/shard_map/ppermute | solution.py:268
  179.7 2.5 %collective-permute-start.23 = (bf16[128,2048]{1,0:T(8,128)(2,1)S(1)}, bf16[128,2048]{1,0:T(8,128)(2,1)S(1)}, u32[]{:S(2)}, u32[]{:S(2)}) collective-permute-start(bf16[128,2048]{1,0:T(8,128)(2,1)S(1)} %fusion.15), channel_id=1, source_target_pairs={{0,30},{2,28},{4,26},{6,24},{8,22},{10,20},{12,18},{14,16},{16,14}... | collective-permute-start | bytes 1572872 | tf_op jit(solution)/shard_map/ppermute | solution.py:268
  182.3 13.5 %collective-permute-done.17 = bf16[128,2048]{1,0:T(8,128)(2,1)S(1)} collective-permute-done((bf16[128,2048]{1,0:T(8,128)(2,1)S(1)}, bf16[128,2048]{1,0:T(8,128)(2,1)S(1)}, u32[]{:S(2)}, u32[]{:S(2)}) %collective-permute-start.17) | collective-permute-done | bytes 524320 | tf_op jit(solution)/shard_map/ppermute | solution.py:268
  197.5 41.7 %collective-permute-done.20 = bf16[128,2048]{1,0:T(8,128)(2,1)S(1)} collective-permute-done((bf16[128,2048]{1,0:T(8,128)(2,1)S(1)}, bf16[128,2048]{1,0:T(8,128)(2,1)S(1)}, u32[]{:S(2)}, u32[]{:S(2)}) %collective-permute-start.20) | collective-permute-done | bytes 524320 | tf_op jit(solution)/shard_map/ppermute | solution.py:268
  241.7 8.1 %collective-permute-done.23 = bf16[128,2048]{1,0:T(8,128)(2,1)S(1)} collective-permute-done((bf16[128,2048]{1,0:T(8,128)(2,1)S(1)}, bf16[128,2048]{1,0:T(8,128)(2,1)S(1)}, u32[]{:S(2)}, u32[]{:S(2)}) %collective-permute-start.23) | collective-permute-done | bytes 524320 | tf_op jit(solution)/shard_map/ppermute | solution.py:268
  (81 shorter events, 23.2 us)
Async XLA Ops:
  1.9 10.3 %collective-permute-start = (bf16[3,16,2048]{2,1,0:T(8,128)(2,1)S(1)}, bf16[3,16,2048]{2,1,0:T(8,128)(2,1)S(1)}, u32[]{:S(2)}, u32[]{:S(2)}) collective-permute-start(bf16[3,16,2048]{2,1,0:T(8,128)(2,1)S(1)} %pad_maximum_fusion), channel_id=1, source_target_pairs={{0,2},{2,4},{4,6},{6,8},{8,10},{10,12},{12,14},{14,16},{16,18},{18... | collective-permute-start | bytes 589832 | tf_op jit(solution)/shard_map/ppermute | solution.py:216
  23.7 15.4 %collective-permute-start.1 = (bf16[1,128,2048]{2,1,0:T(8,128)(2,1)S(1)}, bf16[1,128,2048]{2,1,0:T(8,128)(2,1)S(1)}, u32[]{:S(2)}, u32[]{:S(2)}) collective-permute-start(bf16[1,128,2048]{2,1,0:T(8,128)(2,1)S(1)} %get-tuple-element.22), channel_id=1, source_target_pairs={{0,1},{1,0},{2,3},{3,2},{4,5},{5,4},{6,7},{7,6},{8,9},{9,8},{10,11... | collective-permute-start | bytes 1572872 | tf_op jit(solution)/shard_map/ppermute | solution.py:254
  38.5 13.9 %collective-permute-start.3 = (bf16[2,128,2048]{2,1,0:T(8,128)(2,1)S(1)}, bf16[2,128,2048]{2,1,0:T(8,128)(2,1)S(1)}, u32[]{:S(2)}, u32[]{:S(2)}) collective-permute-start(bf16[2,128,2048]{2,1,0:T(8,128)(2,1)S(1)} %get-tuple-element.24), channel_id=1, source_target_pairs={{0,1},{1,0},{2,3},{3,2},{4,5},{5,4},{6,7},{7,6},{8,9},{9,8},{10,11... | collective-permute-start | bytes 3145736 | tf_op jit(solution)/shard_map/ppermute | solution.py:254
  39.3 39.6 %collective-permute-start.2 = (bf16[128,2048]{1,0:T(8,128)(2,1)S(1)}, bf16[128,2048]{1,0:T(8,128)(2,1)S(1)}, u32[]{:S(2)}, u32[]{:S(2)}) collective-permute-start(bf16[128,2048]{1,0:T(8,128)(2,1)S(1)} %fusion.rest_0_), channel_id=1, source_target_pairs={{0,16},{2,18},{4,20},{6,22},{8,24},{10,26},{12,28},{14,30},{16,0},... | collective-permute-start | bytes 1572872 | tf_op jit(solution)/shard_map/ppermute | solution.py:268
  52.4 27.4 %collective-permute-start.6 = (bf16[2,128,2048]{2,1,0:T(8,128)(2,1)S(1)}, bf16[2,128,2048]{2,1,0:T(8,128)(2,1)S(1)}, u32[]{:S(2)}, u32[]{:S(2)}) collective-permute-start(bf16[2,128,2048]{2,1,0:T(8,128)(2,1)S(1)} %get-tuple-element.26), channel_id=1, source_target_pairs={{0,1},{1,0},{2,3},{3,2},{4,5},{5,4},{6,7},{7,6},{8,9},{9,8},{10,11... | collective-permute-start | bytes 3145736 | tf_op jit(solution)/shard_map/ppermute | solution.py:254
  52.9 42.5 %collective-permute-start.4 = (bf16[128,2048]{1,0:T(8,128)(2,1)S(1)}, bf16[128,2048]{1,0:T(8,128)(2,1)S(1)}, u32[]{:S(2)}, u32[]{:S(2)}) collective-permute-start(bf16[128,2048]{1,0:T(8,128)(2,1)S(1)} %get-tuple-element.49.rest_0_), channel_id=1, source_target_pairs={{0,18},{2,16},{4,22},{6,20},{8,26},{10,24},{12,30},{14,28},{16,2},... | collective-permute-start | bytes 1572872 | tf_op jit(solution)/shard_map/ppermute | solution.py:268
  54.0 42.2 %collective-permute-start.5 = (bf16[128,2048]{1,0:T(8,128)(2,1)S(1)}, bf16[128,2048]{1,0:T(8,128)(2,1)S(1)}, u32[]{:S(2)}, u32[]{:S(2)}) collective-permute-start(bf16[128,2048]{1,0:T(8,128)(2,1)S(1)} %get-tuple-element.48.rest_1_), channel_id=1, source_target_pairs={{0,2},{2,0},{4,6},{6,4},{8,10},{10,8},{12,14},{14,12},{16,18},{18,... | collective-permute-start | bytes 1572872 | tf_op jit(solution)/shard_map/ppermute | solution.py:268
  78.8 29.4 %collective-permute-start.9 = (bf16[3,128,2048]{2,1,0:T(8,128)(2,1)S(1)}, bf16[3,128,2048]{2,1,0:T(8,128)(2,1)S(1)}, u32[]{:S(2)}, u32[]{:S(2)}) collective-permute-start(bf16[3,128,2048]{2,1,0:T(8,128)(2,1)S(1)} %get-tuple-element.28), channel_id=1, source_target_pairs={{0,1},{1,0},{2,3},{3,2},{4,5},{5,4},{6,7},{7,6},{8,9},{9,8},{10,11... | collective-permute-start | bytes 4718600 | tf_op jit(solution)/shard_map/ppermute | solution.py:254
  80.2 26.4 %collective-permute-start.7 = (bf16[128,2048]{1,0:T(8,128)(2,1)S(1)}, bf16[128,2048]{1,0:T(8,128)(2,1)S(1)}, u32[]{:S(2)}, u32[]{:S(2)}) collective-permute-start(bf16[128,2048]{1,0:T(8,128)(2,1)S(1)} %get-tuple-element.47.rest_0_), channel_id=1, source_target_pairs={{0,20},{2,22},{4,16},{6,18},{8,28},{10,30},{12,24},{14,26},{16,4},... | collective-permute-start | bytes 1572872 | tf_op jit(solution)/shard_map/ppermute | solution.py:268
  80.2 27.1 %collective-permute-start.8 = (bf16[128,2048]{1,0:T(8,128)(2,1)S(1)}, bf16[128,2048]{1,0:T(8,128)(2,1)S(1)}, u32[]{:S(2)}, u32[]{:S(2)}) collective-permute-start(bf16[128,2048]{1,0:T(8,128)(2,1)S(1)} %get-tuple-element.46.rest_1_), channel_id=1, source_target_pairs={{0,4},{2,6},{4,0},{6,2},{8,12},{10,14},{12,8},{14,10},{16,20},{18,... | collective-permute-start | bytes 1572872 | tf_op jit(solution)/shard_map/ppermute | solution.py:268
  95.3 19.0 %collective-permute-start.13 = (bf16[2,128,2048]{2,1,0:T(8,128)(2,1)S(1)}, bf16[2,128,2048]{2,1,0:T(8,128)(2,1)S(1)}, u32[]{:S(2)}, u32[]{:S(2)}) collective-permute-start(bf16[2,128,2048]{2,1,0:T(8,128)(2,1)S(1)} %get-tuple-element.30), channel_id=1, source_target_pairs={{0,1},{1,0},{2,3},{3,2},{4,5},{5,4},{6,7},{7,6},{8,9},{9,8},{10,11... | collective-permute-start | bytes 3145736 | tf_op jit(solution)/shard_map/ppermute | solution.py:254
  108.8 44.3 %collective-permute-start.10 = (bf16[128,2048]{1,0:T(8,128)(2,1)S(1)}, bf16[128,2048]{1,0:T(8,128)(2,1)S(1)}, u32[]{:S(2)}, u32[]{:S(2)}) collective-permute-start(bf16[128,2048]{1,0:T(8,128)(2,1)S(1)} %get-tuple-element.41.rest_0_), channel_id=1, source_target_pairs={{0,22},{2,20},{4,18},{6,16},{8,30},{10,28},{12,26},{14,24},{16,6},... | collective-permute-start | bytes 1572872 | tf_op jit(solution)/shard_map/ppermute | solution.py:268
  111.2 42.8 %collective-permute-start.11 = (bf16[128,2048]{1,0:T(8,128)(2,1)S(1)}, bf16[128,2048]{1,0:T(8,128)(2,1)S(1)}, u32[]{:S(2)}, u32[]{:S(2)}) collective-permute-start(bf16[128,2048]{1,0:T(8,128)(2,1)S(1)} %get-tuple-element.40.rest_1_), channel_id=1, source_target_pairs={{0,6},{2,4},{4,2},{6,0},{8,14},{10,12},{12,10},{14,8},{16,22},{18,... | collective-permute-start | bytes 1572872 | tf_op jit(solution)/shard_map/ppermute | solution.py:268
  114.4 41.0 %collective-permute-start.12 = (bf16[128,2048]{1,0:T(8,128)(2,1)S(1)}, bf16[128,2048]{1,0:T(8,128)(2,1)S(1)}, u32[]{:S(2)}, u32[]{:S(2)}) collective-permute-start(bf16[128,2048]{1,0:T(8,128)(2,1)S(1)} %get-tuple-element.39.rest_2_), channel_id=1, source_target_pairs={{0,8},{2,10},{4,12},{6,14},{8,0},{10,2},{12,4},{14,6},{16,24},{18,... | collective-permute-start | bytes 1572872 | tf_op jit(solution)/shard_map/ppermute | solution.py:268
  114.8 42.8 %collective-permute-start.14 = (bf16[128,2048]{1,0:T(8,128)(2,1)S(1)}, bf16[128,2048]{1,0:T(8,128)(2,1)S(1)}, u32[]{:S(2)}, u32[]{:S(2)}) collective-permute-start(bf16[128,2048]{1,0:T(8,128)(2,1)S(1)} %get-tuple-element.45.rest_0_), channel_id=1, source_target_pairs={{0,24},{2,26},{4,28},{6,30},{8,16},{10,18},{12,20},{14,22},{16,8},... | collective-permute-start | bytes 1572872 | tf_op jit(solution)/shard_map/ppermute | solution.py:268
  117.4 52.7 %collective-permute-start.15 = (bf16[128,2048]{1,0:T(8,128)(2,1)S(1)}, bf16[128,2048]{1,0:T(8,128)(2,1)S(1)}, u32[]{:S(2)}, u32[]{:S(2)}) collective-permute-start(bf16[128,2048]{1,0:T(8,128)(2,1)S(1)} %get-tuple-element.44.rest_1_), channel_id=1, source_target_pairs={{0,10},{2,8},{4,14},{6,12},{8,2},{10,0},{12,6},{14,4},{16,26},{18,... | collective-permute-start | bytes 1572872 | tf_op jit(solution)/shard_map/ppermute | solution.py:268
  153.1 5.3 %collective-permute-start.16 = (bf16[2,128,2048]{2,1,0:T(8,128)(2,1)S(1)}, bf16[2,128,2048]{2,1,0:T(8,128)(2,1)S(1)}, u32[]{:S(2)}, u32[]{:S(2)}) collective-permute-start(bf16[2,128,2048]{2,1,0:T(8,128)(2,1)S(1)} %get-tuple-element.32), channel_id=1, source_target_pairs={{0,1},{1,0},{2,3},{3,2},{4,5},{5,4},{6,7},{7,6},{8,9},{9,8},{10,11... | collective-permute-start | bytes 3145736 | tf_op jit(solution)/shard_map/ppermute | solution.py:254
  154.0 20.0 %collective-permute-start.19 = (bf16[3,128,2048]{2,1,0:T(8,128)(2,1)S(1)}, bf16[3,128,2048]{2,1,0:T(8,128)(2,1)S(1)}, u32[]{:S(2)}, u32[]{:S(2)}) collective-permute-start(bf16[3,128,2048]{2,1,0:T(8,128)(2,1)S(1)} %get-tuple-element.34), channel_id=1, source_target_pairs={{0,1},{1,0},{2,3},{3,2},{4,5},{5,4},{6,7},{7,6},{8,9},{9,8},{10,11... | collective-permute-start | bytes 4718600 | tf_op jit(solution)/shard_map/ppermute | solution.py:254
  170.1 9.6 %collective-permute-start.22 = (bf16[1,128,2048]{2,1,0:T(8,128)(2,1)S(1)}, bf16[1,128,2048]{2,1,0:T(8,128)(2,1)S(1)}, u32[]{:S(2)}, u32[]{:S(2)}) collective-permute-start(bf16[1,128,2048]{2,1,0:T(8,128)(2,1)S(1)} %get-tuple-element.36), channel_id=1, source_target_pairs={{0,1},{1,0},{2,3},{3,2},{4,5},{5,4},{6,7},{7,6},{8,9},{9,8},{10,11... | collective-permute-start | bytes 1572872 | tf_op jit(solution)/shard_map/ppermute | solution.py:254
  171.0 24.8 %collective-permute-start.17 = (bf16[128,2048]{1,0:T(8,128)(2,1)S(1)}, bf16[128,2048]{1,0:T(8,128)(2,1)S(1)}, u32[]{:S(2)}, u32[]{:S(2)}) collective-permute-start(bf16[128,2048]{1,0:T(8,128)(2,1)S(1)} %get-tuple-element.43.rest_0_), channel_id=1, source_target_pairs={{0,26},{2,24},{4,30},{6,28},{8,18},{10,16},{12,22},{14,20},{16,10}... | collective-permute-start | bytes 1572872 | tf_op jit(solution)/shard_map/ppermute | solution.py:268
  174.0 22.7 %collective-permute-start.18 = (bf16[128,2048]{1,0:T(8,128)(2,1)S(1)}, bf16[128,2048]{1,0:T(8,128)(2,1)S(1)}, u32[]{:S(2)}, u32[]{:S(2)}) collective-permute-start(bf16[128,2048]{1,0:T(8,128)(2,1)S(1)} %get-tuple-element.42.rest_1_), channel_id=1, source_target_pairs={{0,12},{2,14},{4,8},{6,10},{8,4},{10,6},{12,0},{14,2},{16,28},{18,... | collective-permute-start | bytes 1572872 | tf_op jit(solution)/shard_map/ppermute | solution.py:268
  174.4 64.8 %collective-permute-start.20 = (bf16[128,2048]{1,0:T(8,128)(2,1)S(1)}, bf16[128,2048]{1,0:T(8,128)(2,1)S(1)}, u32[]{:S(2)}, u32[]{:S(2)}) collective-permute-start(bf16[128,2048]{1,0:T(8,128)(2,1)S(1)} %get-tuple-element.38), channel_id=1, source_target_pairs={{0,28},{2,30},{4,24},{6,26},{8,20},{10,22},{12,16},{14,18},{16,12}... | collective-permute-start | bytes 1572872 | tf_op jit(solution)/shard_map/ppermute | solution.py:268
  175.1 64.9 %collective-permute-start.21 = (bf16[128,2048]{1,0:T(8,128)(2,1)S(1)}, bf16[128,2048]{1,0:T(8,128)(2,1)S(1)}, u32[]{:S(2)}, u32[]{:S(2)}) collective-permute-start(bf16[128,2048]{1,0:T(8,128)(2,1)S(1)} %get-tuple-element.37), channel_id=1, source_target_pairs={{0,14},{2,12},{4,10},{6,8},{8,6},{10,4},{12,2},{14,0},{16,30},{18,... | collective-permute-start | bytes 1572872 | tf_op jit(solution)/shard_map/ppermute | solution.py:268
  179.7 70.1 %collective-permute-start.23 = (bf16[128,2048]{1,0:T(8,128)(2,1)S(1)}, bf16[128,2048]{1,0:T(8,128)(2,1)S(1)}, u32[]{:S(2)}, u32[]{:S(2)}) collective-permute-start(bf16[128,2048]{1,0:T(8,128)(2,1)S(1)} %fusion.15), channel_id=1, source_target_pairs={{0,30},{2,28},{4,26},{6,24},{8,22},{10,20},{12,18},{14,16},{16,14}... | collective-permute-start | bytes 1572872 | tf_op jit(solution)/shard_map/ppermute | solution.py:268
  (5 other events, 43.0 us)
